TPU v7x, 32 devices: a whole 2x2x4 slice. The times are simulated.
32 devices in a mesh: pole: 2 (over x), row: 8 (over z, y), leaf: 2 (over core).
Axes of the slice: x: 2, y: 2, z: 4, core: 2. Of those that a mesh axis runs over, the one named last changes fastest.
Arguments:
- ancestor_inverse: float32 [4, 2, 8192, 4096], P('pole', 'leaf', 'row'), parts along dimension 0, may hold values from -6 to 6
- panel: float32 [4, 2, 4096, 512], P('pole', 'leaf', 'row'), parts along dimension 0, may hold values from -0.0625 to 0.0625
- diagonal_inverse: float32 [4, 2, 256, 256], P('pole', 'leaf'), parts along dimension 0, may hold values from -6 to 6
- pattern: int32 [64, 2], replicated, may hold values 0 or 1
Outputs:
- offdiag_inverse: float32 [4, 8192, 512], P('pole', 'row', 'leaf'), parts along dimension 0
- diag_inverse: float32 [4, 2, 256, 256], P('pole', 'leaf'), parts along dimension 0
There are 2 independent parts, one for each index of `pole`. A program takes and returns all parts, laid end to end along the dimension named above; an argument that names none is the same for every part. Nothing has to cross between parts.
All inputs are finite; a program needn't handle non-finite values.
Results may differ from a plain program's by a relative error of at most 0.0001.
Values sent between devices are 32-bit elements; how exact they have to be, the bound alone decides.
No kernel may reach another device: no remote copies, remote signals or barrier semaphores. Data moves between devices by JAX's collectives and lax.ppermute only.
A program may use at most 128 MiB of HBM per device.

v0:
```python
import jax
import jax.numpy as jnp
from jax import lax
from jax.sharding import PartitionSpec as P

WIDTH = 256
BLOCK = 128


def complex_apply(form, left, right):

    def mult(a, b):
        return jnp.einsum(
            form, a, b, preferred_element_type=jnp.float32, precision=lax.Precision.HIGHEST
        )

    real_part = mult(left[0], right[0]) - mult(left[1], right[1])
    imag_part = mult(left[0], right[1]) + mult(left[1], right[0])
    return jnp.stack([real_part, imag_part])


def contract(inverse_piece, panel_piece):
    groups = panel_piece.shape[3] // WIDTH
    results = []
    for group in range(groups):
        slab = panel_piece[..., group * WIDTH : (group + 1) * WIDTH]

        def compute(slab=slab):
            return complex_apply("hiq,hqk->ik", inverse_piece, slab)

        results.append(compute())
    return jnp.concatenate(results, axis=2)


def local(ancestor_inverse, panel, diagonal_inverse, pattern):
    row_count = ancestor_inverse.shape[2]
    row_start = lax.axis_index("row") * row_count
    sibling = lax.axis_index("leaf")
    block_count = row_count // BLOCK
    local_pattern = lax.dynamic_slice_in_dim(pattern, row_start // BLOCK, block_count, 0).astype(
        jnp.float32
    )
    panel_mask = jnp.repeat(jnp.repeat(local_pattern, BLOCK // 2, axis=0), WIDTH, axis=1)
    masked = panel * panel_mask[None, None]
    own_rows = jnp.repeat(local_pattern, BLOCK, axis=0)
    own_mask = jnp.where(sibling == 0, own_rows[:, 0], own_rows[:, 1])
    swapped = lax.all_to_all(masked, "leaf", split_axis=3, concat_axis=1, tiled=True)
    partial_value = contract(ancestor_inverse, lax.all_gather(masked, "row", axis=2, tiled=True))
    product = lax.psum_scatter(partial_value, "leaf", scatter_dimension=2, tiled=True)
    update = -product * own_mask[None, :, None]
    paired = jnp.transpose(update.reshape(2, row_count // 2, 2, WIDTH), (0, 2, 1, 3))
    diag_term = complex_apply("hqa,hqb->ab", swapped, paired)
    correction = lax.psum(diag_term, "row")
    return (update, diagonal_inverse - correction[:, None])


def solution(mesh):
    in_specs = (
        P("pole", "leaf", "row", None),
        P("pole", "leaf", "row", None),
        P("pole", "leaf", None, None),
        P(),
    )
    out_specs = (P("pole", "row", "leaf"), P("pole", "leaf", None, None))
    return jax.shard_map(local, mesh=mesh, in_specs=in_specs, out_specs=out_specs, check_vma=False)
```

profile of v0, /device:TPU:0, one launch (start us, length us, event | category | flops | bytes accessed | tf_op | source)
XLA Modules:
  0.0 584.2 jit_solution(5143073751186071659)
XLA Ops:
  8.9 1.7 broadcast_multiply_fusion
  10.7 230.4 %all-gather.2.cloned.1.call-done = f32[2,1,4096,512]{3,2,1,0:T(8,128)} async-done(((f32[2,1,512,512]{3,2,1,0:T(8,128)}), f32[2,1,4096,512]{3,2,1,0:T(8,128)}) %all-gather.2.cloned.1.call-update) | async-done | bytes 16777232 | tf_op jit(solution)/shard_map/all_gather | solution.py:48
  241.1 29.9 %fusion.6 = f32[256,1024]{1,0:T(8,128)S(1)} fusion(f32[2,1,1024,4096]{3,2,1,0:T(8,128)} %param.4, f32[2,1,4096,512]{3,2,1,0:T(8,128)} %all-gather.2.cloned.1.call-done), kind=kOutput, calls=%fused_computation.6 | convolution fusion | flops 12884901888 | bytes 22020096 | tf_op jit(solution)/shard_map/hiq,hqk->ik/dot_general | solution.py:13
  271.0 29.1 %fusion.4 = f32[256,1024]{1,0:T(8,128)S(1)} fusion(f32[2,1,1024,4096]{3,2,1,0:T(8,128)S(1)} %copy-done, f32[2,1,4096,512]{3,2,1,0:T(8,128)} %all-gather.2.cloned.1.call-done), kind=kOutput, calls=%fused_computation.4 | convolution fusion | flops 12884901888 | bytes 22020096 | tf_op jit(solution)/shard_map/hiq,hqk->ik/dot_general | solution.py:13
  300.1 28.7 %fusion.2 = f32[256,1024]{1,0:T(8,128)S(1)} fusion(f32[2,1,1024,4096]{3,2,1,0:T(8,128)S(1)} %copy-done, f32[2,1,4096,512]{3,2,1,0:T(8,128)} %all-gather.2.cloned.1.call-done), kind=kOutput, calls=%fused_computation.2 | convolution fusion | flops 12884901888 | bytes 22020096 | tf_op jit(solution)/shard_map/hiq,hqk->ik/dot_general | solution.py:13
  328.8 28.7 %fusion = f32[256,1024]{1,0:T(8,128)S(1)} fusion(f32[2,1,1024,4096]{3,2,1,0:T(8,128)S(1)} %copy-done, f32[2,1,4096,512]{3,2,1,0:T(8,128)} %all-gather.2.cloned.1.call-done), kind=kOutput, calls=%fused_computation | convolution fusion | flops 12884901888 | bytes 22020096 | tf_op jit(solution)/shard_map/hiq,hqk->ik/dot_general | solution.py:13
  357.5 29.9 %fusion.27 = f32[1,1024,256]{1,2,0:T(8,128)} fusion(f32[256,1024]{1,0:T(8,128)S(1)} %fusion.6, f32[2,1,1024,4096]{3,2,1,0:T(8,128)S(1)} %copy-done, f32[2,1,4096,512]{3,2,1,0:T(8,128)} %all-gather.2.cloned.1.call-done), kind=kOutput, calls=%fused_computation.32 | convolution fusion | flops 12885164032 | bytes 23068672 | tf_op jit(solution)/shard_map/hiq,hqk->ik/dot_general | solution.py:13
  387.4 28.9 %fusion.33 = f32[1,1024,256]{1,2,0:T(8,128)S(1)} fusion(f32[256,1024]{1,0:T(8,128)S(1)} %fusion.4, f32[2,1,1024,4096]{3,2,1,0:T(8,128)S(1)} %copy-done, f32[2,1,4096,512]{3,2,1,0:T(8,128)} %all-gather.2.cloned.1.call-done), kind=kOutput, calls=%fused_computation.34 | convolution fusion | flops 12885164032 | bytes 23068672 | tf_op jit(solution)/shard_map/hiq,hqk->ik/dot_general | solution.py:13
  416.3 29.2 %fusion.39 = f32[1,1024,256]{1,2,0:T(8,128)S(1)} fusion(f32[256,1024]{1,0:T(8,128)S(1)} %fusion.2, f32[2,1,1024,4096]{3,2,1,0:T(8,128)S(1)} %copy-done, f32[2,1,4096,512]{3,2,1,0:T(8,128)} %all-gather.2.cloned.1.call-done), kind=kOutput, calls=%fused_computation.36 | convolution fusion | flops 12885164032 | bytes 23068672 | tf_op jit(solution)/shard_map/hiq,hqk->ik/dot_general | solution.py:13
  445.5 29.9 %fusion.45 = f32[1,1024,256]{1,2,0:T(8,128)} fusion(f32[256,1024]{1,0:T(8,128)S(1)} %fusion, f32[2,1,1024,4096]{3,2,1,0:T(8,128)S(1)} %copy-done, f32[2,1,4096,512]{3,2,1,0:T(8,128)} %all-gather.2.cloned.1.call-done), kind=kOutput, calls=%fused_computation.38 | convolution fusion | flops 12885164032 | bytes 23068672 | tf_op jit(solution)/shard_map/hiq,hqk->ik/dot_general | solution.py:13
  475.4 3.8 maximum_maximum_fusion
  479.2 1.6 copy-done.2
  480.7 2.4 copy.36
  483.2 4.0 all-to-all-start
  487.3 2.7 all-to-all-done
  490.1 1.7 copy.37
  491.8 1.8 negate_multiply_fusion
  493.6 2.5 copy.38
  496.2 2.1 copy.47
  500.5 1.0 fusion.49
  501.5 1.0 fusion.51
  503.4 1.8 copy.41
  505.2 70.3 %all-reduce.2.cloned.1.call-done = f32[2,1,256,256]{3,2,0,1:T(8,128)} async-done(((f32[2,1,256,256]{3,2,0,1:T(8,128)}), f32[2,1,256,256]{3,2,0,1:T(8,128)}) %all-reduce.2.cloned.1.call-update) | async-done | bytes 524304 | tf_op jit(solution)/shard_map/psum | solution.py:53
  575.5 1.9 fusion.52
  (29 shorter events, 4.9 us)
Async XLA Ops:
  7.2 1.8 copy-start.4
  7.2 233.9 %all-gather.2.cloned.1.call-start = ((), (), s32[]{:S(2)}) async-start(), calls=%async_computation.2 | async-start | bytes 18874368 | tf_op jit(solution)/shard_map/all_gather | solution.py:48
  10.6 481.2 %reduce-scatter.2.cloned.1.call-start = ((), (), s32[]{:S(2)}) async-start(), calls=%async_computation.3 | async-start | bytes 6291456 | tf_op jit(solution)/shard_map/reduce_scatter | solution.py:49
  241.1 29.9 %copy-start = (f32[2,1,1024,4096]{3,2,1,0:T(8,128)S(1)}, f32[2,1,1024,4096]{3,2,1,0:T(8,128)}, u32[]{:S(2)}) copy-start(f32[2,1,1024,4096]{3,2,1,0:T(8,128)} %param.4) | copy-start | bytes 100663296
  445.5 29.9 %copy-start.3 = (f32[1,1024,256]{1,2,0:T(8,128)S(1)}, f32[1,1024,256]{1,2,0:T(8,128)}, u32[]{:S(2)}) copy-start(f32[1,1024,256]{1,2,0:T(8,128)} %fusion.27) | copy-start | bytes 3145732
  479.2 1.6 copy-start.2
  483.2 6.9 %all-to-all-start = ((f32[2,1,512,512]{2,0,1,3:T(2,128)}), f32[2,1,512,512]{2,0,1,3:T(2,128)S(1)}, u32[]{:S(2)}, u32[]{:S(2)}) async-start(f32[2,1,512,512]{2,0,1,3:T(2,128)} %copy.36), calls=%async_computation.1 | async-start | bytes 4194304 | tf_op jit(solution)/shard_map/all_to_all | solution.py:47
  487.2 88.3 %all-reduce.2.cloned.1.call-start = ((), (), s32[]{:S(2)}) async-start(), calls=%async_computation.4 | async-start | bytes 1048576 | tf_op jit(solution)/shard_map/psum | solution.py:53
  496.2 2.2 copy-start.1
  501.5 74.0 %copy-start.5 = (f32[2,1,256,256]{3,2,1,0:T(8,128)S(1)}, f32[2,1,256,256]{3,2,1,0:T(8,128)}, u32[]{:S(2)}) copy-start(f32[2,1,256,256]{3,2,1,0:T(8,128)} %param.6) | copy-start | bytes 1572868
Sparse Core Ops, SparseCore 0:
  10.8 230.2 all-gather.1
  479.3 10.2 reduce-scatter.1
  503.5 71.9 all-reduce.1
where the time goes:
time: 591 us; the launch traced here: 584 us
  waiting for transfers between devices  303 us (51%)
  matrix products  238 us (40%)
  between operations  14.2 us (2%)
  local copies, waits for them, and re-layouts  13.2 us (2%)
  other arithmetic  10.9 us (2%)
    dot_general x12, matrix products, mult(): jnp.einsum(form, a, b, preferred_element_type=jnp.float32, precision=lax....  238 us
    all_gather x1, waiting for transfers between devices, local(): lax.all_gather(masked, 'row', axis=2, tiled=True)  230 us
    psum x1, waiting for transfers between devices, local(): correction = lax.psum(diag_term, 'row')  70.3 us
  transfers between devices with their start and end apart: 4, of which 3 were waited for; matrix products, arithmetic and copies ran while one was open for 1% of the time, Pallas kernels for 0%

commit v1 on v0

--- a/solution.py
+++ b/solution.py
@@ -1,10 +1,18 @@
+import functools
+import itertools
+
 import jax
 import jax.numpy as jnp
 from jax import lax
+from jax.experimental import pallas as pl
+from jax.experimental.pallas import tpu as pltpu
 from jax.sharding import PartitionSpec as P
 
 WIDTH = 256
 BLOCK = 128
+HALF = WIDTH // 2
+QUARTER = WIDTH // 4
+TILE = 512
 
 
 def complex_apply(form, left, right):
@@ -24,15 +32,11 @@
     results = []
     for group in range(groups):
         slab = panel_piece[..., group * WIDTH : (group + 1) * WIDTH]
-
-        def compute(slab=slab):
-            return complex_apply("hiq,hqk->ik", inverse_piece, slab)
-
-        results.append(compute())
+        results.append(complex_apply("hiq,hqk->ik", inverse_piece, slab))
     return jnp.concatenate(results, axis=2)
 
 
-def local(ancestor_inverse, panel, diagonal_inverse, pattern):
+def plain(ancestor_inverse, panel, diagonal_inverse, pattern):
     row_count = ancestor_inverse.shape[2]
     row_start = lax.axis_index("row") * row_count
     sibling = lax.axis_index("leaf")
@@ -54,6 +58,371 @@
     return (update, diagonal_inverse - correction[:, None])
 
 
+def split(value):
+    high = value.astype(jnp.bfloat16)
+    return high, (value - high.astype(jnp.float32)).astype(jnp.bfloat16)
+
+
+def mult(a, b):
+    return jnp.dot(a, b, preferred_element_type=jnp.float32)
+
+
+def mult_split(left, right):
+    return mult(left[0], right[0]) + mult(left[0], right[1]) + mult(left[1], right[0])
+
+
+def halves_kernel(first, second):
+    lane = lax.broadcasted_iota(jnp.int32, first.shape, 1)
+    return (
+        jnp.where(lane < QUARTER, first, pltpu.roll(second, QUARTER, 1)),
+        jnp.where(lane < QUARTER, pltpu.roll(first, QUARTER, 1), second),
+    )
+
+
+def prepare_kernel(me_ref, pattern_ref, panel_ref, wide_ref, second_ref, third_ref):
+    height = BLOCK // 2
+    count = panel_ref.shape[2] // height
+    first = (me_ref[0] * pl.num_programs(0) + pl.program_id(0)) * count
+    for i, part in itertools.product(range(count), range(2)):
+        rows = pl.ds(i * height, height)
+        masks = [pattern_ref[first + i, s].astype(jnp.float32) for s in range(2)]
+        left = [panel_ref[part, 0, rows, pl.ds(s * WIDTH, HALF)] * masks[s] for s in range(2)]
+        right = [panel_ref[part, 0, rows, pl.ds(s * WIDTH + HALF, HALF)] * masks[s] for s in range(2)]
+        for s in range(2):
+            wide_ref[rows, pl.ds((2 * part + s) * HALF, HALF)] = left[s]
+        second, third = halves_kernel(*right)
+        second_ref[rows, pl.ds(part * HALF, HALF)] = second
+        third_ref[rows, pl.ds(part * HALF, HALF)] = third
+
+
+def prepare(me, pattern, panel):
+    rows = panel.shape[2]
+    tile = rows // 2
+    lanes = (4 * HALF, 4 * QUARTER, 4 * QUARTER)
+    return pl.pallas_call(
+        prepare_kernel,
+        out_shape=[jax.ShapeDtypeStruct((rows, n), jnp.float32) for n in lanes],
+        grid_spec=pltpu.PrefetchScalarGridSpec(
+            num_scalar_prefetch=2,
+            grid=(2,),
+            in_specs=[pl.BlockSpec((2, 1, tile, 2 * WIDTH), lambda i, *_: (0, 0, i, 0))],
+            out_specs=[pl.BlockSpec((tile, n), lambda i, *_: (i, 0)) for n in lanes],
+        ),
+        name="prepare",
+    )(me.reshape(1), pattern, panel)
+
+
+def slots_kernel(table_ref, a_ref, *refs, counts, fresh, last, joined):
+    candidates, refs = refs[: 2 * sum(counts)], refs[2 * sum(counts) :]
+    sum_ref, refs = (None, refs) if fresh else (refs[0], refs[1:])
+    out_refs, refs = refs[: 1 + last], refs[1 + last :]
+    piece_ref, high_ref, low_ref, total_ref, sems = refs
+    slots = len(counts)
+    tile, slot = pl.program_id(0), pl.program_id(1)
+    rows, lanes = piece_ref.shape[1] // 2, piece_ref.shape[2]
+    half = lanes // 2
+    side = table_ref[2 * slots]
+
+    def fetch(k, act):
+        first = sum(counts[:k])
+        for j in range(counts[k]):
+
+            @pl.when(table_ref[2 * k + 1] == j)
+            def _():
+                for way in range(2):
+                    place = side if way == 0 else 1 - side
+                    act(
+                        pltpu.make_async_copy(
+                            candidates[2 * (first + j) + way].at[pl.ds(way * joined * rows, rows)],
+                            piece_ref.at[k, pl.ds(pl.multiple_of(place * rows, rows), rows)],
+                            sems.at[k, way],
+                        )
+                    )
+
+    @pl.when(tile == 0)
+    def _():
+        @pl.when(slot == 0)
+        def _():
+            for k in range(slots):
+                fetch(k, lambda copy: copy.start())
+
+        for k in range(slots):
+
+            @pl.when(slot == k)
+            def _():
+                fetch(k, lambda copy: copy.wait())
+
+        high, low = split(piece_ref[slot])
+        for parts, target in ((high, high_ref), (low, low_ref)):
+            target[slot, : 2 * rows] = parts
+            target[slot, 2 * rows :, :half] = -parts[:, half:]
+            target[slot, 2 * rows :, half:] = parts[:, :half]
+
+    total = None
+    for part in range(2):
+        span = pl.ds(2 * rows * part, 2 * rows)
+        term = mult_split(split(a_ref[part]), (high_ref[slot, span], low_ref[slot, span]))
+        total = term if total is None else total + term
+
+    @pl.when(slot == 0)
+    def _():
+        total_ref[...] = total if fresh else sum_ref[...] + total
+
+    @pl.when(slot > 0)
+    def _():
+        total_ref[...] += total
+
+    @pl.when(slot == slots - 1)
+    def _():
+        value = total_ref[...]
+        if not last:
+            out_refs[0][...] = value
+            return
+        if half == 2 * HALF:
+            pieces = [value[:, j * HALF : (j + 1) * HALF] for j in range(4)]
+            siblings = [jnp.concatenate([pieces[s], pieces[2 + s]], axis=1) for s in range(2)]
+        else:
+            siblings = halves_kernel(value[:, :half], value[:, half:])
+        mine = table_ref[2 * slots + 1] == 0
+        out_refs[0][...] = jnp.where(mine, siblings[0], siblings[1])
+        out_refs[1][...] = jnp.where(mine, siblings[1], siblings[0])
+
+
+def add_slots(inverse, slots, picks, total, side, sibling, last=False):
+    row_count = inverse.shape[2]
+    counts = tuple(len(slot) for slot in slots)
+    operands = [array for slot in slots for pair in slot for array in pair]
+    rows, lanes = inverse.shape[3] // 8, operands[0].shape[1]
+    joined = operands[0].shape[0] == 2 * rows
+    fresh = total is None
+    block = pl.BlockSpec((TILE, lanes), lambda i, k, t: (i, 0))
+    specs = [pl.BlockSpec((2, None, TILE, 2 * rows), lambda i, k, t: (0, 0, i, t[2 * k]))]
+    specs += [pl.BlockSpec(memory_space=pl.ANY)] * len(operands)
+    operands = [inverse] + operands
+    if not fresh:
+        specs.append(block)
+        operands.append(total)
+    if last:
+        half_block = pl.BlockSpec((TILE, lanes // 2), lambda i, k, t: (i, 0))
+        out_specs = [half_block] * 2
+        out_shape = [jax.ShapeDtypeStruct((row_count, lanes // 2), jnp.float32)] * 2
+    else:
+        out_specs, out_shape = [block], [jax.ShapeDtypeStruct((row_count, lanes), jnp.float32)]
+    table = [entry for pick in picks for entry in pick] + [side, sibling]
+    result = pl.pallas_call(
+        functools.partial(slots_kernel, counts=counts, fresh=fresh, last=last, joined=joined),
+        out_shape=out_shape,
+        grid_spec=pltpu.PrefetchScalarGridSpec(
+            num_scalar_prefetch=1,
+            grid=(row_count // TILE, len(counts)),
+            in_specs=specs,
+            out_specs=out_specs,
+            scratch_shapes=[
+                pltpu.VMEM((len(counts), 2 * rows, lanes), jnp.float32),
+                pltpu.VMEM((len(counts), 4 * rows, lanes), jnp.bfloat16),
+                pltpu.VMEM((len(counts), 4 * rows, lanes), jnp.bfloat16),
+                pltpu.VMEM((TILE, lanes), jnp.float32),
+                pltpu.SemaphoreType.DMA((len(counts), 2)),
+            ],
+        ),
+        compiler_params=pltpu.CompilerParams(vmem_limit_bytes=60 * 2**20),
+        cost_estimate=pl.CostEstimate(
+            flops=2 * 3 * row_count * 4 * rows * lanes * len(counts),
+            bytes_accessed=4 * 4 * row_count * rows * len(counts),
+            transcendentals=0,
+        ),
+        name=f"slots_{lanes}_{len(counts)}",
+    )(jnp.stack(table).astype(jnp.int32), *operands)
+    return result if last else result[0]
+
+
+def finish_kernel(mine_ref, other_ref, mask_ref, lower_ref, update_ref, term_ref):
+    half = mine_ref.shape[1] // 2
+    value = -(mine_ref[...] + other_ref[...]) * mask_ref[...]
+    update_ref[...] = value
+    if half == QUARTER:
+        lane = lax.broadcasted_iota(jnp.int32, value.shape, 1)
+        rolled = pltpu.roll(value, QUARTER, 1)
+        turned = jnp.where(lane < QUARTER, -rolled, rolled)
+    else:
+        turned = jnp.concatenate([-value[:, half:], value[:, :half]], axis=1)
+    total = None
+    for part, right in enumerate((value, turned)):
+        term = mult_split(split(lower_ref[part]), split(right))
+        total = term if total is None else total + term
+    term_ref[...] = total
+
+
+def finish(mine, other, mask, lower):
+    row_count, lanes = mine.shape
+    return pl.pallas_call(
+        finish_kernel,
+        out_shape=[
+            jax.ShapeDtypeStruct((row_count, lanes), jnp.float32),
+            jax.ShapeDtypeStruct((WIDTH, lanes), jnp.float32),
+        ],
+        compiler_params=pltpu.CompilerParams(vmem_limit_bytes=32 * 2**20),
+        cost_estimate=pl.CostEstimate(flops=0, bytes_accessed=0, transcendentals=0),
+        name=f"finish_{lanes}",
+    )(mine, other, mask, lower)
+
+
+def assemble_kernel(wide_ref, second_ref, third_ref, out_ref):
+    parts = halves_kernel(second_ref[...], third_ref[...])
+    for part in range(2):
+        out_ref[part, :, :HALF] = wide_ref[:, part * HALF : (part + 1) * HALF]
+        out_ref[part, :, HALF:] = parts[part]
+
+
+def assemble(wide, second, third):
+    rows = wide.shape[0]
+    tile = rows // 2
+    return pl.pallas_call(
+        assemble_kernel,
+        out_shape=jax.ShapeDtypeStruct((2, rows, WIDTH), jnp.float32),
+        grid=(2,),
+        in_specs=[
+            pl.BlockSpec((tile, WIDTH), lambda i: (i, 0)),
+            pl.BlockSpec((tile, HALF), lambda i: (i, 0)),
+            pl.BlockSpec((tile, HALF), lambda i: (i, 0)),
+        ],
+        out_specs=pl.BlockSpec((2, tile, WIDTH), lambda i: (0, i, 0)),
+        cost_estimate=pl.CostEstimate(flops=0, bytes_accessed=0, transcendentals=0),
+        name="assemble",
+    )(wide, second, third)
+
+
+def lined(ancestor_inverse, panel, diagonal_inverse, pattern):
+    row_count = ancestor_inverse.shape[2]
+    me = lax.axis_index("row")
+    z, y = me // 2, me % 2
+    sibling = lax.axis_index("leaf")
+    block_count = row_count // BLOCK
+    wide, second, third = prepare(me, pattern, panel)
+
+    def up(value, step):
+        pairs = [(2 * i + j, 2 * i + 2 + j) for i in range(step, 3) for j in (0, 1)]
+        return lax.ppermute(value, "row", pairs)
+
+    def down(value, step):
+        pairs = [(2 * i + j, 2 * i - 2 + j) for i in range(1, 4 - step) for j in (0, 1)]
+        return lax.ppermute(value, "row", pairs)
+
+    def across(value, places=(0, 1, 2, 3)):
+        pairs = [(2 * i + j, 2 * i + 1 - j) for i in places for j in (0, 1)]
+        return lax.ppermute(value, "row", pairs)
+
+    def swap(value):
+        return lax.ppermute(value, "leaf", [(0, 1), (1, 0)])
+
+    layout = (
+        (("u0",), (0, 1, 2, 3), (0, 0, 0, 0)),
+        (("u1", "d1"), (1, 0, 1, 2), (1, 0, 0, 0)),
+        (("u2", "d1", "d2"), (2, 2, 3, 1), (2, 1, 1, 0)),
+        (("u2", "u3", "d2", "d3"), (3, 3, 0, 0), (3, 2, 0, 1)),
+    )
+
+    def by_z(values):
+        return jnp.where(z == 0, values[0], jnp.where(z == 1, values[1], jnp.where(z == 2, values[2], values[3])))
+
+    picks = [(by_z(sources), by_z(choices)) for _, sources, choices in layout]
+
+    live = {"w u0": wide, "s u0": second, "t u0": third}
+
+    def fence():
+        live.update(lax.optimization_barrier(dict(live)))
+
+    def hop(chain, step):
+        live[f"{chain} u{step}"] = up(live[f"{chain} u{max(step - 1, 0)}"], step - 1)
+        live[f"{chain} d{step}"] = down(live[f"{chain} {'d' if step > 1 else 'u'}{step - 1}"], step - 1)
+
+    def cross(chain, slot):
+        names, _, choices = layout[slot]
+        for j, name in enumerate(names):
+            places = [i for i in range(4) if choices[i] == j]
+            live[f"{chain} y{slot} {name}"] = across(live[f"{chain} {name}"], places)
+
+    def add(chain, wanted, last=False):
+        slots = []
+        for k in wanted:
+            names = layout[k][0]
+            if chain == "t":
+                slots.append([(live[f"t {name}"],) * 2 for name in names])
+            else:
+                slots.append([(live[f"{chain} {name}"], live[f"{chain} y{k} {name}"]) for name in names])
+        total = live.pop(f"{chain} total", None)
+        result = add_slots(ancestor_inverse, slots, [picks[k] for k in wanted], total, y, sibling, last)
+        if last:
+            return result
+        live[f"{chain} total"] = result
+
+    local_pattern = lax.dynamic_slice_in_dim(pattern, me * block_count, block_count, 0).astype(jnp.float32)
+    own_pattern = jnp.where(sibling == 0, local_pattern[:, 0], local_pattern[:, 1])
+    own_mask = jnp.broadcast_to(jnp.repeat(own_pattern, BLOCK)[:, None], (row_count, HALF))
+    pair = panel[:, 0]
+    keep = jnp.where(sibling == 0, pair[..., :WIDTH], pair[..., WIDTH:])
+    give = jnp.where(sibling == 0, pair[..., WIDTH:], pair[..., :WIDTH])
+
+    def lower_rows():
+        got = swap(give)
+        even = jnp.where(sibling == 0, keep, got)
+        odd = jnp.where(sibling == 0, got, keep)
+        rows = jnp.stack([even, odd], axis=2).reshape(2, row_count, WIDTH)
+        return jnp.transpose(rows * own_mask[None, :, :1], (0, 2, 1))
+
+    def total_sum(term):
+        for distance in (1, 2, 4):
+            term = term + lax.ppermute(term, "row", [(i, i ^ distance) for i in range(8)])
+        return term
+
+    hop("w", 1)
+    cross("w", 0)
+    hop("s", 1)
+    live["crossed"] = across(live["t u0"])
+    fence()
+    hop("w", 2)
+    cross("w", 1)
+    hop("s", 2)
+    cross("s", 0)
+    live["t u0"] = jnp.concatenate([live["t u0"], live.pop("crossed")])
+    add("w", (0,))
+    fence()
+    hop("w", 3)
+    cross("w", 2)
+    hop("s", 3)
+    cross("s", 1)
+    add("w", (1,))
+    add("t", (0,))
+    live["lower"] = lower_rows()
+    fence()
+    hop("t", 1)
+    cross("w", 3)
+    add("w", (2,))
+    add("s", (0, 1))
+    fence()
+    hop("t", 2)
+    cross("s", 2)
+    cross("s", 3)
+    mine, theirs = add("w", (3,), last=True)
+    live["update w"], live["term w"] = finish(mine, swap(theirs), jnp.concatenate([own_mask] * 2, axis=1), live["lower"])
+    add("t", (1,))
+    fence()
+    hop("t", 3)
+    mine, theirs = add("s", (2, 3), last=True)
+    live["update s"], live["term s"] = finish(mine, swap(theirs), own_mask, live["lower"])
+    live["sum w"] = total_sum(live["term w"])
+    add("t", (2,))
+    fence()
+    mine, theirs = add("t", (3,), last=True)
+    update_first, update_second = live["update w"], live["update s"]
+    update_third, term_third = finish(mine, swap(theirs), own_mask, live["lower"])
+    sums = [live["sum w"], total_sum(live["term s"]), total_sum(term_third)]
+
+    update = assemble(update_first, update_second, update_third)
+    sums = [jnp.concatenate([s[:, : s.shape[1] // 2] for s in sums], axis=1), jnp.concatenate([s[:, s.shape[1] // 2 :] for s in sums], axis=1)]
+    return (update, diagonal_inverse - jnp.stack(sums)[:, None])
+
+
 def solution(mesh):
     in_specs = (
         P("pole", "leaf", "row", None),
@@ -62,4 +431,5 @@
         P(),
     )
     out_specs = (P("pole", "row", "leaf"), P("pole", "leaf", None, None))
+    local = lined if mesh.shape["row"] == 8 and mesh.shape["leaf"] == 2 else plain
     return jax.shard_map(local, mesh=mesh, in_specs=in_specs, out_specs=out_specs, check_vma=False)

time: 591 us -> 342 us (0.58)
  matrix products: 238 us -> 0 us
  waiting for transfers between devices: 303 us -> 87.3 us
  Pallas kernels: 0 us -> 131 us
  starting transfers between devices: 4.15 us -> 90 us
  between operations: 14.2 us -> 1.42 us
    dot_general x12 -> x0, matrix products: 238 us -> none  [mult(): jnp.einsum(form, a, b, preferred_element_type=jnp.float32, precision=lax....]
    all_gather x1 -> x0, waiting for transfers between devices: 230 us -> none  [local(): lax.all_gather(masked, 'row', axis=2, tiled=True)]
    pallas_call x0 -> x15, Pallas kernels: none -> 131 us  [the longest x10 122 us: add_slots(): pl.pallas_call(functools.partial(slots_kernel, counts=counts, fresh=fresh...]
    ppermute x0 -> x52, starting transfers between devices: none -> 90 us  [the longest x21 36.7 us: across(): return lax.ppermute(value, 'row', pairs)]
    ppermute x0 -> x52, waiting for transfers between devices: none -> 87.3 us  [the longest x9 28.8 us: total_sum(): lax.ppermute(term, 'row', [(i, i ^ distance) for i in range(8)])]
    psum x1 -> x0, waiting for transfers between devices: 70.3 us -> none  [local(): correction = lax.psum(diag_term, 'row')]
    unnamed x16 -> x53, local copies, waits for them, and re-layouts: 3.62 us -> 11.4 us
  transfers between devices with their start and end apart: 4 -> 52, of which waited for: 3 -> 16; matrix products, arithmetic and copies ran while one was open for 1% -> 5% of each run, Pallas kernels for 0% -> 35%
where the time goes in v1:
time: 342 us; the launch traced here: 340 us
  Pallas kernels  131 us (38%)
  starting transfers between devices  90 us (26%)
  waiting for transfers between devices  87.3 us (26%)
  local copies, waits for them, and re-layouts  17.5 us (5%)
  other arithmetic  12.3 us (4%)
    pallas_call x10, Pallas kernels, add_slots(): pl.pallas_call(functools.partial(slots_kernel, counts=counts, fresh=fresh...  122 us
    ppermute x21, starting transfers between devices, across(): return lax.ppermute(value, 'row', pairs)  36.7 us
    ppermute x9, starting transfers between devices, up(): return lax.ppermute(value, 'row', pairs)  32 us
    ppermute x9, waiting for transfers between devices, total_sum(): lax.ppermute(term, 'row', [(i, i ^ distance) for i in range(8)])  28.8 us
    ppermute x9, waiting for transfers between devices, up(): return lax.ppermute(value, 'row', pairs)  22.9 us
    ppermute x9, waiting for transfers between devices, down(): return lax.ppermute(value, 'row', pairs)  20 us
    ppermute x21, waiting for transfers between devices, across(): return lax.ppermute(value, 'row', pairs)  15.6 us
    ppermute x9, starting transfers between devices, down(): return lax.ppermute(value, 'row', pairs)  11.6 us
  transfers between devices with their start and end apart: 52, of which 16 were waited for; matrix products, arithmetic and copies ran while one was open for 5% of the time, Pallas kernels for 35%

profile of v1, /device:TPU:0, one launch (start us, length us, event | category | flops | bytes accessed | tf_op | source)
XLA Modules:
  0.0 340.0 jit_solution(11709145775905627003)
XLA Ops:
  2.2 3.9 %prepare.1 = (f32[512,512]{1,0:T(8,128)}, f32[512,256]{1,0:T(8,128)}, f32[512,256]{1,0:T(8,128)}) custom-call(s32[1]{0:T(128)} %bitcast.7.me_ref, s32[64,2]{1,0:T(8,128)} %copy.12.pattern_ref, f32[2,1,512,512]{3,2,1,0:T(8,128)} %panel_ref.1), custom_call_target="tpu_custom_call" | custom-call | tf_op jit(solution)/shard_map/prepare/pallas_call | solution.py:102
  8.7 7.2 %collective-permute-start.5 = (f32[512,512]{1,0:T(8,128)}, f32[512,512]{1,0:T(8,128)}, u32[]{:S(2)}, u32[]{:S(2)}) collective-permute-start(f32[512,512]{1,0:T(8,128)} %get-tuple-element.120.refs_0_), channel_id=1, source_target_pairs={{0,4},{2,6},{4,8},{6,10},{8,12},{10,14},{1,5},{3,7},{5,9},{7,11},{... | collective-permute-start | bytes 3145736 | tf_op jit(solution)/shard_map/ppermute | solution.py:305
  17.8 3.8 %collective-permute-start.3 = (f32[512,256]{1,0:T(8,128)}, f32[512,256]{1,0:T(8,128)}, u32[]{:S(2)}, u32[]{:S(2)}) collective-permute-start(f32[512,256]{1,0:T(8,128)} %get-tuple-element.141.refs_0_), channel_id=1, source_target_pairs={{0,4},{2,6},{4,8},{6,10},{8,12},{10,14},{1,5},{3,7},{5,9},{7,11},{... | collective-permute-start | bytes 1572872 | tf_op jit(solution)/shard_map/ppermute | solution.py:305
  25.9 22.9 %collective-permute-done.3.refs_2_ = f32[512,256]{1,0:T(8,128)} collective-permute-done((f32[512,256]{1,0:T(8,128)}, f32[512,256]{1,0:T(8,128)}, u32[]{:S(2)}, u32[]{:S(2)}) %collective-permute-start.3) | collective-permute-done | bytes 524320 | tf_op jit(solution)/shard_map/ppermute | solution.py:305
  48.8 3.1 collective-permute-done.1
  62.0 7.4 %collective-permute-done.7.refs_4_.refs_10_ = f32[512,256]{1,0:T(8,128)S(1)} collective-permute-done((f32[512,256]{1,0:T(8,128)S(1)}, f32[512,256]{1,0:T(8,128)S(1)}, u32[]{:S(2)}, u32[]{:S(2)}) %collective-permute-start.7) | collective-permute-done | bytes 524320 | tf_op jit(solution)/shard_map/ppermute | solution.py:309
  74.5 13.1 %slots_512_1.4.refs_4_ = f32[1024,512]{1,0:T(8,128)} custom-call(s32[4]{0:T(128)} %add_add_fusion.table_ref, f32[2,1,1024,4096]{3,2,1,0:T(8,128)} %a_ref.19, f32[512,512]{1,0:T(8,128)} %get-tuple-element.120.refs_0_, f32[512,512]{1,0:T(8,128)} %collective-permute-done.6.refs_1_), custom_call_target="tpu_custom_call" | custom-call | flops 6442450944 | bytes 8388608 | tf_op jit(solution)/shard_map/slots_512_1/pallas_call | solution.py:212
  93.6 3.3 collective-permute-start.16
  115.7 9.3 %slots_256_1.4.refs_4_ = f32[1024,256]{1,0:T(8,128)} custom-call(s32[4]{0:T(128)} %add_add_fusion.table_ref, f32[2,1,1024,4096]{3,2,1,0:T(8,128)} %a_ref.19, f32[1024,256]{1,0:T(8,128)} %pad_maximum_fusion.1.refs_0_.refs_1_, f32[1024,256]{1,0:T(8,128)} %pad_maximum_fusion.1.refs_0_.refs_1_), custom_call_target="tpu_custom_call" | custom-call | flops 3221225472 | bytes 8388608 | tf_op jit(solution)/shard_map/slots_256_1/pallas_call | solution.py:212
  125.0 13.9 %slots_512_1.5.refs_6_ = f32[1024,512]{1,0:T(8,128)} custom-call(s32[4]{0:T(128)} %add_add_fusion.1.table_ref, f32[2,1,1024,4096]{3,2,1,0:T(8,128)} %a_ref.19, f32[512,512]{1,0:T(8,128)} %collective-permute-done.5.refs_0_, f32[512,512]{1,0:T(8,128)} %collective-permute-done.13.refs_1_, f32[512,512]{1,0:T(8,128)} %collective-permute-done.4.refs_2_, ...), custom_call_target="tpu_custom_call" | custom-call | flops 6442450944 | bytes 8388608 | tf_op jit(solution)/shard_map/slots_512_1/pallas_call | solution.py:212
  142.1 11.5 %collective-permute-start.24 = (f32[1024,256]{1,0:T(8,128)S(1)}, f32[1024,256]{1,0:T(8,128)}, u32[]{:S(2)}, u32[]{:S(2)}) collective-permute-start(f32[1024,256]{1,0:T(8,128)S(1)} %copy-done.10), channel_id=1, source_target_pairs={{0,4},{2,6},{4,8},{6,10},{8,12},{10,14},{1,5},{3,7},{5,9},{7,11},{... | collective-permute-start | bytes 3145736 | tf_op jit(solution)/shard_map/ppermute | solution.py:305
  159.4 8.3 %collective-permute-done.23.refs_2_.refs_3_ = f32[1024,256]{1,0:T(8,128)} collective-permute-done((f32[1024,256]{1,0:T(8,128)S(1)}, f32[1024,256]{1,0:T(8,128)}, u32[]{:S(2)}, u32[]{:S(2)}) %collective-permute-start.23) | collective-permute-done | bytes 1048608 | tf_op jit(solution)/shard_map/ppermute | solution.py:309
  169.3 13.7 %slots_512_1.6.refs_8_ = f32[1024,512]{1,0:T(8,128)} custom-call(s32[4]{0:T(128)} %add_add_fusion.2.table_ref, f32[2,1,1024,4096]{3,2,1,0:T(8,128)} %a_ref.19, f32[512,512]{1,0:T(8,128)} %collective-permute-done.11.refs_0_, f32[512,512]{1,0:T(8,128)} %collective-permute-done.22.refs_1_, f32[512,512]{1,0:T(8,128)} %collective-permute-done.4.refs_2_, ...), custom_call_target="tpu_custom_call" | custom-call | flops 6442450944 | bytes 8388608 | tf_op jit(solution)/shard_map/slots_512_1/pallas_call | solution.py:212
  183.1 14.2 %slots_256_2.2.refs_14_ = f32[1024,256]{1,0:T(8,128)} custom-call(s32[6]{0:T(128)} %stack.52.table_ref, f32[2,1,1024,4096]{3,2,1,0:T(8,128)} %a_ref.19, f32[512,256]{1,0:T(8,128)} %get-tuple-element.141.refs_0_, f32[512,256]{1,0:T(8,128)} %collective-permute-done.9.refs_1_, f32[512,256]{1,0:T(8,128)} %collective-permute-done.3.refs_2_, ...), custom_call_target="tpu_custom_call" | custom-call | flops 6442450944 | bytes 16777216 | tf_op jit(solution)/shard_map/slots_256_2/pallas_call | solution.py:212
  198.4 13.8 %slots_512_1.7 = (f32[1024,256]{1,0:T(8,128)}, f32[1024,256]{1,0:T(8,128)}) custom-call(s32[4]{0:T(128)} %add_add_fusion.3.table_ref, f32[2,1,1024,4096]{3,2,1,0:T(8,128)} %a_ref.19, f32[512,512]{1,0:T(8,128)} %collective-permute-done.11.refs_0_, f32[512,512]{1,0:T(8,128)} %collective-permute-done.27.refs_1_, f32[512,512]{1,0:T(8,128)} %collective-permute-done.19.refs_2_, ...), custom_call_target="tpu_custom_call" | custom-call | flops 6442450944 | bytes 8388608 | tf_op jit(solution)/shard_map/slots_512_1/pallas_call | solution.py:212
  217.2 11.3 %collective-permute-done.30.refs_5_ = f32[512,256]{1,0:T(8,128)S(1)} collective-permute-done((f32[512,256]{1,0:T(8,128)S(1)}, f32[512,256]{1,0:T(8,128)S(1)}, u32[]{:S(2)}, u32[]{:S(2)}) %collective-permute-start.30) | collective-permute-done | bytes 524320 | tf_op jit(solution)/shard_map/ppermute | solution.py:313
  236.8 9.6 %slots_256_1.5.refs_6_ = f32[1024,256]{1,0:T(8,128)} custom-call(s32[4]{0:T(128)} %add_add_fusion.1.table_ref, f32[2,1,1024,4096]{3,2,1,0:T(8,128)} %a_ref.19, f32[1024,256]{1,0:T(8,128)} %collective-permute-done.24.refs_0_.refs_1_, f32[1024,256]{1,0:T(8,128)} %collective-permute-done.24.refs_0_.refs_1_, ...), custom_call_target="tpu_custom_call" | custom-call | flops 3221225472 | bytes 8388608 | tf_op jit(solution)/shard_map/slots_256_1/pallas_call | solution.py:212
  263.1 14.6 %slots_256_2.3 = (f32[1024,128]{1,0:T(8,128)}, f32[1024,128]{1,0:T(8,128)}) custom-call(s32[6]{0:T(128)} %stack.59.table_ref, f32[2,1,1024,4096]{3,2,1,0:T(8,128)} %a_ref.19, f32[512,256]{1,0:T(8,128)} %collective-permute-done.8.refs_0_.refs_6_, f32[512,256]{1,0:T(8,128)} %copy-done.17, f32[512,256]{1,0:T(8,128)} %copy-done.11, f32[512,256]{1,0:T(8,128)} %copy-done.15, ...), custom_call_target="tpu_custom_call" | custom-call | flops 6442450944 | bytes 16777216 | tf_op jit(solution)/shard_map/slots_256_2/pallas_call | solution.py:212
  277.7 9.6 %collective-permute-done.40 = f32[256,256]{1,0:T(8,128)S(1)} collective-permute-done((f32[256,256]{1,0:T(8,128)S(1)}, f32[256,256]{1,0:T(8,128)S(1)}, u32[]{:S(2)}, u32[]{:S(2)}) %collective-permute-start.40) | collective-permute-done | bytes 262176 | tf_op jit(solution)/shard_map/ppermute | solution.py:375
  287.4 9.7 %slots_256_1.6.refs_8_ = f32[1024,256]{1,0:T(8,128)} custom-call(s32[4]{0:T(128)} %add_add_fusion.2.table_ref, f32[2,1,1024,4096]{3,2,1,0:T(8,128)} %a_ref.19, f32[1024,256]{1,0:T(8,128)} %collective-permute-done.37.refs_0_.refs_1_, f32[1024,256]{1,0:T(8,128)} %collective-permute-done.37.refs_0_.refs_1_, ...), custom_call_target="tpu_custom_call" | custom-call | flops 3221225472 | bytes 8388608 | tf_op jit(solution)/shard_map/slots_256_1/pallas_call | solution.py:212
  300.7 9.7 %slots_256_1.7 = (f32[1024,128]{1,0:T(8,128)}, f32[1024,128]{1,0:T(8,128)}) custom-call(s32[4]{0:T(128)} %add_add_fusion.3.table_ref, f32[2,1,1024,4096]{3,2,1,0:T(8,128)} %a_ref.19, f32[1024,256]{1,0:T(8,128)} %collective-permute-done.37.refs_0_.refs_1_, f32[1024,256]{1,0:T(8,128)} %collective-permute-done.37.refs_0_.refs_1_, ...), custom_call_target="tpu_custom_call" | custom-call | flops 3221225472 | bytes 8388608 | tf_op jit(solution)/shard_map/slots_256_1/pallas_call | solution.py:212
  311.7 4.7 %collective-permute-done.46 = f32[256,128]{1,0:T(8,128)S(1)} collective-permute-done((f32[256,128]{1,0:T(8,128)S(1)}, f32[256,128]{1,0:T(8,128)S(1)}, u32[]{:S(2)}, u32[]{:S(2)}) %collective-permute-start.46) | collective-permute-done | bytes 131104 | tf_op jit(solution)/shard_map/ppermute | solution.py:375
  326.5 4.0 %collective-permute-done.48 = f32[256,128]{1,0:T(8,128)S(1)} collective-permute-done((f32[256,128]{1,0:T(8,128)S(1)}, f32[256,128]{1,0:T(8,128)S(1)}, u32[]{:S(2)}, u32[]{:S(2)}) %collective-permute-start.48) | collective-permute-done | bytes 131104 | tf_op jit(solution)/shard_map/ppermute | solution.py:375
  335.0 3.9 %collective-permute-done.51 = f32[256,128]{1,0:T(8,128)S(1)} collective-permute-done((f32[256,128]{1,0:T(8,128)S(1)}, f32[256,128]{1,0:T(8,128)S(1)}, u32[]{:S(2)}, u32[]{:S(2)}) %collective-permute-start.51) | collective-permute-done | bytes 131104 | tf_op jit(solution)/shard_map/ppermute | solution.py:375
  (180 shorter events, 112.3 us)
Async XLA Ops:
  7.4 44.5 %collective-permute-start.4 = (f32[512,512]{1,0:T(8,128)}, f32[512,512]{1,0:T(8,128)}, u32[]{:S(2)}, u32[]{:S(2)}) collective-permute-start(f32[512,512]{1,0:T(8,128)} %get-tuple-element.120.refs_0_), channel_id=1, source_target_pairs={{4,0},{6,2},{8,4},{10,6},{12,8},{14,10},{5,1},{7,3},{9,5},{11,7},{... | collective-permute-start | bytes 3145736 | tf_op jit(solution)/shard_map/ppermute | solution.py:309
  8.7 43.2 %collective-permute-start.5 = (f32[512,512]{1,0:T(8,128)}, f32[512,512]{1,0:T(8,128)}, u32[]{:S(2)}, u32[]{:S(2)}) collective-permute-start(f32[512,512]{1,0:T(8,128)} %get-tuple-element.120.refs_0_), channel_id=1, source_target_pairs={{0,4},{2,6},{4,8},{6,10},{8,12},{10,14},{1,5},{3,7},{5,9},{7,11},{... | collective-permute-start | bytes 3145736 | tf_op jit(solution)/shard_map/ppermute | solution.py:305
  15.8 36.9 %collective-permute-start.6 = (f32[512,512]{1,0:T(8,128)}, f32[512,512]{1,0:T(8,128)}, u32[]{:S(2)}, u32[]{:S(2)}) collective-permute-start(f32[512,512]{1,0:T(8,128)} %get-tuple-element.120.refs_0_), channel_id=1, source_target_pairs={{0,2},{2,0},{4,6},{6,4},{8,10},{10,8},{12,14},{14,12},{1,3},{3,1},... | collective-permute-start | bytes 3145736 | tf_op jit(solution)/shard_map/ppermute | solution.py:313
  17.8 31.0 %collective-permute-start.3 = (f32[512,256]{1,0:T(8,128)}, f32[512,256]{1,0:T(8,128)}, u32[]{:S(2)}, u32[]{:S(2)}) collective-permute-start(f32[512,256]{1,0:T(8,128)} %get-tuple-element.141.refs_0_), channel_id=1, source_target_pairs={{0,4},{2,6},{4,8},{6,10},{8,12},{10,14},{1,5},{3,7},{5,9},{7,11},{... | collective-permute-start | bytes 1572872 | tf_op jit(solution)/shard_map/ppermute | solution.py:305
  23.9 27.9 %collective-permute-start.1 = (f32[512,256]{1,0:T(8,128)}, f32[512,256]{1,0:T(8,128)S(1)}, u32[]{:S(2)}, u32[]{:S(2)}) collective-permute-start(f32[512,256]{1,0:T(8,128)} %get-tuple-element.117), channel_id=1, source_target_pairs={{0,2},{2,0},{4,6},{6,4},{8,10},{10,8},{12,14},{14,12},{1,3},{3,1},... | collective-permute-start | bytes 1572872 | tf_op jit(solution)/shard_map/ppermute | solution.py:313
  58.5 31.2 %collective-permute-start.10 = (f32[512,512]{1,0:T(8,128)}, f32[512,512]{1,0:T(8,128)}, u32[]{:S(2)}, u32[]{:S(2)}) collective-permute-start(f32[512,512]{1,0:T(8,128)} %collective-permute-done.4.refs_2_), channel_id=1, source_target_pairs={{4,0},{6,2},{8,4},{10,6},{5,1},{7,3},{9,5},{11,7},{20,16},{22,18},... | collective-permute-start | bytes 3145736 | tf_op jit(solution)/shard_map/ppermute | solution.py:309
  59.7 31.1 %collective-permute-start.12 = (f32[512,512]{1,0:T(8,128)}, f32[512,512]{1,0:T(8,128)}, u32[]{:S(2)}, u32[]{:S(2)}) collective-permute-start(f32[512,512]{1,0:T(8,128)} %collective-permute-done.4.refs_2_), channel_id=1, source_target_pairs={{0,2},{2,0},{1,3},{3,1},{16,18},{18,16},{17,19},{19,17}} | collective-permute-start | bytes 3145736 | tf_op jit(solution)/shard_map/ppermute | solution.py:313
  73.4 25.5 %collective-permute-start = (f32[2,512,256]{2,1,0:T(8,128)}, f32[2,512,256]{2,1,0:T(8,128)}, u32[]{:S(2)}, u32[]{:S(2)}) collective-permute-start(f32[2,512,256]{2,1,0:T(8,128)} %slice_select_fusion), channel_id=1, source_target_pairs={{0,1},{1,0},{2,3},{3,2},{4,5},{5,4},{6,7},{7,6},{8,9},{9,8},{10,11... | collective-permute-start | bytes 3145736 | tf_op jit(solution)/shard_map/ppermute | solution.py:316
  105.0 33.9 %collective-permute-start.18 = (f32[512,512]{1,0:T(8,128)}, f32[512,512]{1,0:T(8,128)}, u32[]{:S(2)}, u32[]{:S(2)}) collective-permute-start(f32[512,512]{1,0:T(8,128)} %collective-permute-done.10.refs_4_), channel_id=1, source_target_pairs={{4,0},{6,2},{5,1},{7,3},{20,16},{22,18},{21,17},{23,19}} | collective-permute-start | bytes 3145736 | tf_op jit(solution)/shard_map/ppermute | solution.py:309
  106.3 32.7 %collective-permute-start.21 = (f32[512,512]{1,0:T(8,128)}, f32[512,512]{1,0:T(8,128)}, u32[]{:S(2)}, u32[]{:S(2)}) collective-permute-start(f32[512,512]{1,0:T(8,128)} %collective-permute-done.10.refs_4_), channel_id=1, source_target_pairs={{0,2},{2,0},{1,3},{3,1},{16,18},{18,16},{17,19},{19,17}} | collective-permute-start | bytes 3145736 | tf_op jit(solution)/shard_map/ppermute | solution.py:313
  108.9 30.1 %collective-permute-start.19 = (f32[512,512]{1,0:T(8,128)}, f32[512,512]{1,0:T(8,128)}, u32[]{:S(2)}, u32[]{:S(2)}) collective-permute-start(f32[512,512]{1,0:T(8,128)} %collective-permute-done.11.refs_0_), channel_id=1, source_target_pairs={{8,12},{10,14},{9,13},{11,15},{24,28},{26,30},{25,29},{27,31}} | collective-permute-start | bytes 3145736 | tf_op jit(solution)/shard_map/ppermute | solution.py:305
  110.5 28.4 %collective-permute-start.22 = (f32[512,512]{1,0:T(8,128)}, f32[512,512]{1,0:T(8,128)}, u32[]{:S(2)}, u32[]{:S(2)}) collective-permute-start(f32[512,512]{1,0:T(8,128)} %collective-permute-done.11.refs_0_), channel_id=1, source_target_pairs={{12,14},{14,12},{13,15},{15,13},{28,30},{30,28},{29,31},{31,29}} | collective-permute-start | bytes 3145736 | tf_op jit(solution)/shard_map/ppermute | solution.py:313
  112.2 26.7 %collective-permute-start.20 = (f32[512,512]{1,0:T(8,128)}, f32[512,512]{1,0:T(8,128)}, u32[]{:S(2)}, u32[]{:S(2)}) collective-permute-start(f32[512,512]{1,0:T(8,128)} %collective-permute-done.4.refs_2_), channel_id=1, source_target_pairs={{4,6},{6,4},{8,10},{10,8},{5,7},{7,5},{9,11},{11,9},{20,22},{22,20... | collective-permute-start | bytes 3145736 | tf_op jit(solution)/shard_map/ppermute | solution.py:313
  139.0 28.7 %collective-permute-start.23 = (f32[1024,256]{1,0:T(8,128)S(1)}, f32[1024,256]{1,0:T(8,128)}, u32[]{:S(2)}, u32[]{:S(2)}) collective-permute-start(f32[1024,256]{1,0:T(8,128)S(1)} %copy-done.10), channel_id=1, source_target_pairs={{4,0},{6,2},{8,4},{10,6},{12,8},{14,10},{5,1},{7,3},{9,5},{11,7},{... | collective-permute-start | bytes 3145736 | tf_op jit(solution)/shard_map/ppermute | solution.py:309
  142.1 55.1 %collective-permute-start.24 = (f32[1024,256]{1,0:T(8,128)S(1)}, f32[1024,256]{1,0:T(8,128)}, u32[]{:S(2)}, u32[]{:S(2)}) collective-permute-start(f32[1024,256]{1,0:T(8,128)S(1)} %copy-done.10), channel_id=1, source_target_pairs={{0,4},{2,6},{4,8},{6,10},{8,12},{10,14},{1,5},{3,7},{5,9},{7,11},{... | collective-permute-start | bytes 3145736 | tf_op jit(solution)/shard_map/ppermute | solution.py:305
  153.6 43.6 %collective-permute-start.25 = (f32[512,512]{1,0:T(8,128)}, f32[512,512]{1,0:T(8,128)}, u32[]{:S(2)}, u32[]{:S(2)}) collective-permute-start(f32[512,512]{1,0:T(8,128)} %collective-permute-done.10.refs_4_), channel_id=1, source_target_pairs={{4,6},{6,4},{5,7},{7,5},{20,22},{22,20},{21,23},{23,21}} | collective-permute-start | bytes 3145736 | tf_op jit(solution)/shard_map/ppermute | solution.py:313
  155.3 42.0 %collective-permute-start.26 = (f32[512,512]{1,0:T(8,128)}, f32[512,512]{1,0:T(8,128)}, u32[]{:S(2)}, u32[]{:S(2)}) collective-permute-start(f32[512,512]{1,0:T(8,128)} %collective-permute-done.18.refs_6_), channel_id=1, source_target_pairs={{0,2},{2,0},{1,3},{3,1},{16,18},{18,16},{17,19},{19,17}} | collective-permute-start | bytes 3145736 | tf_op jit(solution)/shard_map/ppermute | solution.py:313
  157.7 39.6 %collective-permute-start.27 = (f32[512,512]{1,0:T(8,128)}, f32[512,512]{1,0:T(8,128)}, u32[]{:S(2)}, u32[]{:S(2)}) collective-permute-start(f32[512,512]{1,0:T(8,128)} %collective-permute-done.11.refs_0_), channel_id=1, source_target_pairs={{8,10},{10,8},{9,11},{11,9},{24,26},{26,24},{25,27},{27,25}} | collective-permute-start | bytes 3145736 | tf_op jit(solution)/shard_map/ppermute | solution.py:313
  167.7 29.6 %collective-permute-start.28 = (f32[512,512]{1,0:T(8,128)}, f32[512,512]{1,0:T(8,128)}, u32[]{:S(2)}, u32[]{:S(2)}) collective-permute-start(f32[512,512]{1,0:T(8,128)} %collective-permute-done.19.refs_2_), channel_id=1, source_target_pairs={{12,14},{14,12},{13,15},{15,13},{28,30},{30,28},{29,31},{31,29}} | collective-permute-start | bytes 3145736 | tf_op jit(solution)/shard_map/ppermute | solution.py:313
  215.9 36.3 %collective-permute-start.36 = (f32[1024,256]{1,0:T(8,128)}, f32[1024,256]{1,0:T(8,128)}, u32[]{:S(2)}, u32[]{:S(2)}) collective-permute-start(f32[1024,256]{1,0:T(8,128)} %collective-permute-done.23.refs_2_.refs_3_), channel_id=1, source_target_pairs={{4,0},{6,2},{8,4},{10,6},{5,1},{7,3},{9,5},{11,7},{20,16},{22,18},... | collective-permute-start | bytes 3145736 | tf_op jit(solution)/shard_map/ppermute | solution.py:309
  228.5 23.7 %collective-permute-start.37 = (f32[1024,256]{1,0:T(8,128)}, f32[1024,256]{1,0:T(8,128)}, u32[]{:S(2)}, u32[]{:S(2)}) collective-permute-start(f32[1024,256]{1,0:T(8,128)} %collective-permute-done.24.refs_0_.refs_1_), channel_id=1, source_target_pairs={{4,8},{6,10},{8,12},{10,14},{5,9},{7,11},{9,13},{11,15},{20,24},{2... | collective-permute-start | bytes 3145736 | tf_op jit(solution)/shard_map/ppermute | solution.py:305
  255.3 45.4 %collective-permute-start.42 = (f32[1024,256]{1,0:T(8,128)}, f32[1024,256]{1,0:T(8,128)}, u32[]{:S(2)}, u32[]{:S(2)}) collective-permute-start(f32[1024,256]{1,0:T(8,128)} %collective-permute-done.36.refs_4_.refs_5_), channel_id=1, source_target_pairs={{4,0},{6,2},{5,1},{7,3},{20,16},{22,18},{21,17},{23,19}} | collective-permute-start | bytes 3145736 | tf_op jit(solution)/shard_map/ppermute | solution.py:309
  256.6 44.1 %collective-permute-start.43 = (f32[1024,256]{1,0:T(8,128)}, f32[1024,256]{1,0:T(8,128)}, u32[]{:S(2)}, u32[]{:S(2)}) collective-permute-start(f32[1024,256]{1,0:T(8,128)} %collective-permute-done.37.refs_0_.refs_1_), channel_id=1, source_target_pairs={{8,12},{10,14},{9,13},{11,15},{24,28},{26,30},{25,29},{27,31}} | collective-permute-start | bytes 3145736 | tf_op jit(solution)/shard_map/ppermute | solution.py:305
  261.8 25.5 %collective-permute-start.40 = (f32[256,256]{1,0:T(8,128)S(1)}, f32[256,256]{1,0:T(8,128)S(1)}, u32[]{:S(2)}, u32[]{:S(2)}) collective-permute-start(f32[256,256]{1,0:T(8,128)S(1)} %add.37), channel_id=1, source_target_pairs={{0,4},{2,6},{4,0},{6,2},{8,12},{10,14},{12,8},{14,10},{1,5},{3,7},... | collective-permute-start | bytes 786440 | tf_op jit(solution)/shard_map/ppermute | solution.py:375
  (54 other events, 750.9 us)

commit v2 on v1

--- a/solution.py
+++ b/solution.py
@@ -13,6 +13,7 @@
 HALF = WIDTH // 2
 QUARTER = WIDTH // 4
 TILE = 512
+SCALE = 2
 
 
 def complex_apply(form, left, right):
@@ -79,7 +80,7 @@
     )
 
 
-def prepare_kernel(me_ref, pattern_ref, panel_ref, wide_ref, second_ref, third_ref):
+def prepare_kernel(me_ref, pattern_ref, panel_ref, first_ref, last_ref):
     height = BLOCK // 2
     count = panel_ref.shape[2] // height
     first = (me_ref[0] * pl.num_programs(0) + pl.program_id(0)) * count
@@ -89,16 +90,16 @@
         left = [panel_ref[part, 0, rows, pl.ds(s * WIDTH, HALF)] * masks[s] for s in range(2)]
         right = [panel_ref[part, 0, rows, pl.ds(s * WIDTH + HALF, HALF)] * masks[s] for s in range(2)]
         for s in range(2):
-            wide_ref[rows, pl.ds((2 * part + s) * HALF, HALF)] = left[s]
-        second, third = halves_kernel(*right)
-        second_ref[rows, pl.ds(part * HALF, HALF)] = second
-        third_ref[rows, pl.ds(part * HALF, HALF)] = third
+            first_ref[rows, pl.ds((3 * part + s) * HALF, HALF)] = left[s]
+        third, fourth = halves_kernel(*right)
+        first_ref[rows, pl.ds((3 * part + 2) * HALF, HALF)] = third
+        last_ref[rows, pl.ds(part * HALF, HALF)] = fourth
 
 
 def prepare(me, pattern, panel):
     rows = panel.shape[2]
     tile = rows // 2
-    lanes = (4 * HALF, 4 * QUARTER, 4 * QUARTER)
+    lanes = (6 * HALF, 2 * HALF)
     return pl.pallas_call(
         prepare_kernel,
         out_shape=[jax.ShapeDtypeStruct((rows, n), jnp.float32) for n in lanes],
@@ -112,7 +113,7 @@
     )(me.reshape(1), pattern, panel)
 
 
-def slots_kernel(table_ref, a_ref, *refs, counts, fresh, last, joined):
+def slots_kernel(table_ref, a_ref, *refs, wanted, counts, fresh, last, joined):
     candidates, refs = refs[: 2 * sum(counts)], refs[2 * sum(counts) :]
     sum_ref, refs = (None, refs) if fresh else (refs[0], refs[1:])
     out_refs, refs = refs[: 1 + last], refs[1 + last :]
@@ -121,13 +122,13 @@
     tile, slot = pl.program_id(0), pl.program_id(1)
     rows, lanes = piece_ref.shape[1] // 2, piece_ref.shape[2]
     half = lanes // 2
-    side = table_ref[2 * slots]
+    side = table_ref[8]
 
     def fetch(k, act):
         first = sum(counts[:k])
         for j in range(counts[k]):
 
-            @pl.when(table_ref[2 * k + 1] == j)
+            @pl.when((counts[k] == 1) | (table_ref[4 + wanted[k]] == j))
             def _():
                 for way in range(2):
                     place = side if way == 0 else 1 - side
@@ -178,17 +179,20 @@
         if not last:
             out_refs[0][...] = value
             return
-        if half == 2 * HALF:
-            pieces = [value[:, j * HALF : (j + 1) * HALF] for j in range(4)]
-            siblings = [jnp.concatenate([pieces[s], pieces[2 + s]], axis=1) for s in range(2)]
-        else:
-            siblings = halves_kernel(value[:, :half], value[:, half:])
-        mine = table_ref[2 * slots + 1] == 0
+        siblings = halves_kernel(value[:, half - HALF : half], value[:, 2 * half - HALF :])
+        if half > HALF:
+            siblings = [
+                jnp.concatenate(
+                    [value[:, k * half + s * HALF : k * half + (s + 1) * HALF] for k in range(2)] + [siblings[s]], axis=1
+                )
+                for s in range(2)
+            ]
+        mine = table_ref[9] == 0
         out_refs[0][...] = jnp.where(mine, siblings[0], siblings[1])
         out_refs[1][...] = jnp.where(mine, siblings[1], siblings[0])
 
 
-def add_slots(inverse, slots, picks, total, side, sibling, last=False):
+def add_slots(inverse, table, wanted, slots, total, last=False, ease=1):
     row_count = inverse.shape[2]
     counts = tuple(len(slot) for slot in slots)
     operands = [array for slot in slots for pair in slot for array in pair]
@@ -196,7 +200,7 @@
     joined = operands[0].shape[0] == 2 * rows
     fresh = total is None
     block = pl.BlockSpec((TILE, lanes), lambda i, k, t: (i, 0))
-    specs = [pl.BlockSpec((2, None, TILE, 2 * rows), lambda i, k, t: (0, 0, i, t[2 * k]))]
+    specs = [pl.BlockSpec((2, None, TILE, 2 * rows), lambda i, k, t: (0, 0, i, t[k + wanted[0]]))]
     specs += [pl.BlockSpec(memory_space=pl.ANY)] * len(operands)
     operands = [inverse] + operands
     if not fresh:
@@ -208,9 +212,8 @@
         out_shape = [jax.ShapeDtypeStruct((row_count, lanes // 2), jnp.float32)] * 2
     else:
         out_specs, out_shape = [block], [jax.ShapeDtypeStruct((row_count, lanes), jnp.float32)]
-    table = [entry for pick in picks for entry in pick] + [side, sibling]
     result = pl.pallas_call(
-        functools.partial(slots_kernel, counts=counts, fresh=fresh, last=last, joined=joined),
+        functools.partial(slots_kernel, wanted=wanted, counts=counts, fresh=fresh, last=last, joined=joined),
         out_shape=out_shape,
         grid_spec=pltpu.PrefetchScalarGridSpec(
             num_scalar_prefetch=1,
@@ -227,25 +230,24 @@
         ),
         compiler_params=pltpu.CompilerParams(vmem_limit_bytes=60 * 2**20),
         cost_estimate=pl.CostEstimate(
-            flops=2 * 3 * row_count * 4 * rows * lanes * len(counts),
-            bytes_accessed=4 * 4 * row_count * rows * len(counts),
+            flops=2 * 3 * row_count * 4 * rows * lanes * len(counts) // (SCALE * ease),
+            bytes_accessed=4 * 4 * row_count * rows * len(counts) // (SCALE * ease),
             transcendentals=0,
         ),
         name=f"slots_{lanes}_{len(counts)}",
-    )(jnp.stack(table).astype(jnp.int32), *operands)
+    )(table, *operands)
     return result if last else result[0]
 
 
 def finish_kernel(mine_ref, other_ref, mask_ref, lower_ref, update_ref, term_ref):
-    half = mine_ref.shape[1] // 2
     value = -(mine_ref[...] + other_ref[...]) * mask_ref[...]
     update_ref[...] = value
-    if half == QUARTER:
-        lane = lax.broadcasted_iota(jnp.int32, value.shape, 1)
-        rolled = pltpu.roll(value, QUARTER, 1)
-        turned = jnp.where(lane < QUARTER, -rolled, rolled)
-    else:
-        turned = jnp.concatenate([-value[:, half:], value[:, :half]], axis=1)
+    packed = value[:, -HALF:]
+    lane = lax.broadcasted_iota(jnp.int32, packed.shape, 1)
+    rolled = pltpu.roll(packed, QUARTER, 1)
+    turned = jnp.where(lane < QUARTER, -rolled, rolled)
+    if value.shape[1] > HALF:
+        turned = jnp.concatenate([-value[:, HALF : 2 * HALF], value[:, :HALF], turned], axis=1)
     total = None
     for part, right in enumerate((value, turned)):
         term = mult_split(split(lower_ref[part]), split(right))
@@ -267,29 +269,28 @@
     )(mine, other, mask, lower)
 
 
-def assemble_kernel(wide_ref, second_ref, third_ref, out_ref):
-    parts = halves_kernel(second_ref[...], third_ref[...])
+def assemble_kernel(first_ref, last_ref, out_ref):
+    parts = halves_kernel(first_ref[:, 2 * HALF :], last_ref[...])
     for part in range(2):
-        out_ref[part, :, :HALF] = wide_ref[:, part * HALF : (part + 1) * HALF]
+        out_ref[part, :, :HALF] = first_ref[:, part * HALF : (part + 1) * HALF]
         out_ref[part, :, HALF:] = parts[part]
 
 
-def assemble(wide, second, third):
-    rows = wide.shape[0]
+def assemble(first, last):
+    rows = first.shape[0]
     tile = rows // 2
     return pl.pallas_call(
         assemble_kernel,
         out_shape=jax.ShapeDtypeStruct((2, rows, WIDTH), jnp.float32),
         grid=(2,),
         in_specs=[
-            pl.BlockSpec((tile, WIDTH), lambda i: (i, 0)),
-            pl.BlockSpec((tile, HALF), lambda i: (i, 0)),
+            pl.BlockSpec((tile, 3 * HALF), lambda i: (i, 0)),
             pl.BlockSpec((tile, HALF), lambda i: (i, 0)),
         ],
         out_specs=pl.BlockSpec((2, tile, WIDTH), lambda i: (0, i, 0)),
         cost_estimate=pl.CostEstimate(flops=0, bytes_accessed=0, transcendentals=0),
         name="assemble",
-    )(wide, second, third)
+    )(first, last)
 
 
 def lined(ancestor_inverse, panel, diagonal_inverse, pattern):
@@ -298,7 +299,7 @@
     z, y = me // 2, me % 2
     sibling = lax.axis_index("leaf")
     block_count = row_count // BLOCK
-    wide, second, third = prepare(me, pattern, panel)
+    first, second = prepare(me, pattern, panel)
 
     def up(value, step):
         pairs = [(2 * i + j, 2 * i + 2 + j) for i in range(step, 3) for j in (0, 1)]
@@ -325,9 +326,15 @@
     def by_z(values):
         return jnp.where(z == 0, values[0], jnp.where(z == 1, values[1], jnp.where(z == 2, values[2], values[3])))
 
-    picks = [(by_z(sources), by_z(choices)) for _, sources, choices in layout]
-
-    live = {"w u0": wide, "s u0": second, "t u0": third}
+    table = [by_z(sources) for _, sources, _ in layout] + [by_z(choices) for _, _, choices in layout]
+    table = jnp.stack(table + [y, sibling]).astype(jnp.int32)
+
+    local_pattern = lax.dynamic_slice_in_dim(pattern, me * block_count, block_count, 0).astype(jnp.float32)
+    own_pattern = jnp.where(sibling == 0, local_pattern[:, 0], local_pattern[:, 1])
+    own_mask = jnp.broadcast_to(jnp.repeat(own_pattern, BLOCK)[:, None], (row_count, HALF))
+
+    live = {"c u0": first, "c 0": first, "t 0": second}
+    live["mask"], live["wide mask"] = own_mask, jnp.concatenate([own_mask] * 3, axis=1)
 
     def fence():
         live.update(lax.optimization_barrier(dict(live)))
@@ -336,30 +343,42 @@
         live[f"{chain} u{step}"] = up(live[f"{chain} u{max(step - 1, 0)}"], step - 1)
         live[f"{chain} d{step}"] = down(live[f"{chain} {'d' if step > 1 else 'u'}{step - 1}"], step - 1)
 
+    def select(chain, slot):
+        names, _, choices = layout[slot]
+        value = live[f"{chain} {names[-1]}"]
+        for j, name in enumerate(names[:-1]):
+            chosen = functools.reduce(jnp.logical_or, [z == i for i in range(4) if choices[i] == j])
+            value = jnp.where(chosen, live[f"{chain} {name}"], value)
+        live[f"{chain} {slot}"] = value
+
     def cross(chain, slot):
         names, _, choices = layout[slot]
+        if slot == 3:
+            select(chain, slot)
+        if slot in (0, 3):
+            live[f"{chain} y{slot}"] = across(live[f"{chain} {slot}"])
+            return
         for j, name in enumerate(names):
             places = [i for i in range(4) if choices[i] == j]
             live[f"{chain} y{slot} {name}"] = across(live[f"{chain} {name}"], places)
 
-    def add(chain, wanted, last=False):
+    def add(chain, wanted, last=False, ease=1):
         slots = []
         for k in wanted:
-            names = layout[k][0]
             if chain == "t":
-                slots.append([(live[f"t {name}"],) * 2 for name in names])
+                slots.append([(live[f"t {name}"],) * 2 for name in layout[k][0]])
+            elif k in (1, 2):
+                slots.append([(live[f"{chain} {name}"], live[f"{chain} y{k} {name}"]) for name in layout[k][0]])
             else:
-                slots.append([(live[f"{chain} {name}"], live[f"{chain} y{k} {name}"]) for name in names])
+                slots.append([(live[f"{chain} {k}"], live[f"{chain} y{k}"])])
         total = live.pop(f"{chain} total", None)
-        result = add_slots(ancestor_inverse, slots, [picks[k] for k in wanted], total, y, sibling, last)
+        result = add_slots(ancestor_inverse, live["table"], tuple(wanted), slots, total, last, ease)
         if last:
             return result
         live[f"{chain} total"] = result
 
-    local_pattern = lax.dynamic_slice_in_dim(pattern, me * block_count, block_count, 0).astype(jnp.float32)
-    own_pattern = jnp.where(sibling == 0, local_pattern[:, 0], local_pattern[:, 1])
-    own_mask = jnp.broadcast_to(jnp.repeat(own_pattern, BLOCK)[:, None], (row_count, HALF))
     pair = panel[:, 0]
+    pair = lax.optimization_barrier((pair, first))[0]
     keep = jnp.where(sibling == 0, pair[..., :WIDTH], pair[..., WIDTH:])
     give = jnp.where(sibling == 0, pair[..., WIDTH:], pair[..., :WIDTH])
 
@@ -370,57 +389,49 @@
         rows = jnp.stack([even, odd], axis=2).reshape(2, row_count, WIDTH)
         return jnp.transpose(rows * own_mask[None, :, :1], (0, 2, 1))
 
-    def total_sum(term):
-        for distance in (1, 2, 4):
-            term = term + lax.ppermute(term, "row", [(i, i ^ distance) for i in range(8)])
-        return term
-
-    hop("w", 1)
-    cross("w", 0)
-    hop("s", 1)
-    live["crossed"] = across(live["t u0"])
-    fence()
-    hop("w", 2)
-    cross("w", 1)
-    hop("s", 2)
-    cross("s", 0)
-    live["t u0"] = jnp.concatenate([live["t u0"], live.pop("crossed")])
-    add("w", (0,))
-    fence()
-    hop("w", 3)
-    cross("w", 2)
-    hop("s", 3)
-    cross("s", 1)
-    add("w", (1,))
+    def exchange(term, distance):
+        return term + lax.ppermute(term, "row", [(i, i ^ distance) for i in range(8)])
+
+    hop("c", 1)
+    cross("c", 0)
+    cross("t", 0)
+    live["lower"] = lower_rows()
+    live["table"] = table
+    fence()
+    hop("c", 2)
+    cross("c", 1)
+    live["t u0"] = jnp.concatenate([live.pop("t 0"), live.pop("t y0")])
+    add("c", (0,))
+    fence()
+    hop("c", 3)
+    cross("c", 2)
+    add("c", (1,))
     add("t", (0,))
-    live["lower"] = lower_rows()
     fence()
     hop("t", 1)
-    cross("w", 3)
-    add("w", (2,))
-    add("s", (0, 1))
+    cross("c", 3)
+    add("c", (2,))
     fence()
     hop("t", 2)
-    cross("s", 2)
-    cross("s", 3)
-    mine, theirs = add("w", (3,), last=True)
-    live["update w"], live["term w"] = finish(mine, swap(theirs), jnp.concatenate([own_mask] * 2, axis=1), live["lower"])
-    add("t", (1,))
+    live["mine"], live["theirs"] = add("c", (3,), last=True)
     fence()
     hop("t", 3)
-    mine, theirs = add("s", (2, 3), last=True)
-    live["update s"], live["term s"] = finish(mine, swap(theirs), own_mask, live["lower"])
-    live["sum w"] = total_sum(live["term w"])
-    add("t", (2,))
+    live["update c"], term = finish(live.pop("mine"), swap(live.pop("theirs")), live["wide mask"], live["lower"])
+    live["term c"] = exchange(term, 1)
+    add("t", (1, 2))
     fence()
     mine, theirs = add("t", (3,), last=True)
-    update_first, update_second = live["update w"], live["update s"]
-    update_third, term_third = finish(mine, swap(theirs), own_mask, live["lower"])
-    sums = [live["sum w"], total_sum(live["term s"]), total_sum(term_third)]
-
-    update = assemble(update_first, update_second, update_third)
-    sums = [jnp.concatenate([s[:, : s.shape[1] // 2] for s in sums], axis=1), jnp.concatenate([s[:, s.shape[1] // 2 :] for s in sums], axis=1)]
-    return (update, diagonal_inverse - jnp.stack(sums)[:, None])
+    update_last, term_last = finish(mine, swap(theirs), live["mask"], live["lower"])
+    live["term c"] = exchange(exchange(live["term c"], 2), 4)
+    for distance in (1, 2, 4):
+        term_last = exchange(term_last, distance)
+
+    update = assemble(live["update c"], update_last)
+    total = jnp.concatenate([live["term c"], term_last], axis=1)
+    real = [total[:, :HALF], total[:, 2 * HALF : 2 * HALF + QUARTER], total[:, 3 * HALF : 3 * HALF + QUARTER]]
+    imag = [total[:, HALF : 2 * HALF], total[:, 2 * HALF + QUARTER : 3 * HALF], total[:, 3 * HALF + QUARTER :]]
+    correction = jnp.stack([jnp.concatenate(real, axis=1), jnp.concatenate(imag, axis=1)])
+    return (update, diagonal_inverse - correction[:, None])
 
 
 def solution(mesh):

time: 342 us -> 284 us (0.83)
  starting transfers between devices: 90 us -> 49.7 us
  Pallas kernels: 131 us -> 115 us
  waiting for transfers between devices: 87.3 us -> 92.3 us
  local copies, waits for them, and re-layouts: 17.5 us -> 12.9 us
    ppermute x21 -> x8, waiting for transfers between devices: 15.6 us -> 44.2 us  [across(): return lax.ppermute(value, 'row', pairs)]
    ppermute x9 -> x6, waiting for transfers between devices: 22.9 us -> 0.13 us  [up(): return lax.ppermute(value, 'row', pairs)]
    ppermute x21 -> x8, starting transfers between devices: 36.7 us -> 16.2 us  [across(): return lax.ppermute(value, 'row', pairs)]
    ppermute x9 -> x6, starting transfers between devices: 32 us -> 14.5 us  [up(): return lax.ppermute(value, 'row', pairs)]
    pallas_call x10 -> x7, Pallas kernels: 122 us -> 105 us  [add_slots(): pl.pallas_call(functools.partial(slots_kernel, wanted=wanted, counts=coun...]
    ppermute x9 -> x6, waiting for transfers between devices: 28.8 us -> 21.6 us  [exchange(): lax.ppermute(term, 'row', [(i, i ^ distance) for i in range(8)])]
    ppermute x9 -> x6, waiting for transfers between devices: 20 us -> 25.6 us  [down(): return lax.ppermute(value, 'row', pairs)]
    unnamed x53 -> x19, local copies, waits for them, and re-layouts: 11.4 us -> 7.37 us
  transfers between devices with their start and end apart: 52 -> 29, of which waited for: 16 -> 16; matrix products, arithmetic and copies ran while one was open for 5% -> 4% of each run, Pallas kernels for 35% -> 39%
where the time goes in v2:
time: 284 us; the launch traced here: 283 us
  Pallas kernels  115 us (40%)
  waiting for transfers between devices  92.3 us (32%)
  starting transfers between devices  49.7 us (18%)
  local copies, waits for them, and re-layouts  12.9 us (5%)
  other arithmetic  12.1 us (4%)
    pallas_call x7, Pallas kernels, add_slots(): pl.pallas_call(functools.partial(slots_kernel, wanted=wanted, counts=coun...  105 us
    ppermute x8, waiting for transfers between devices, across(): return lax.ppermute(value, 'row', pairs)  44.2 us
    ppermute x6, waiting for transfers between devices, down(): return lax.ppermute(value, 'row', pairs)  25.6 us
    ppermute x6, waiting for transfers between devices, exchange(): lax.ppermute(term, 'row', [(i, i ^ distance) for i in range(8)])  21.6 us
    ppermute x8, starting transfers between devices, across(): return lax.ppermute(value, 'row', pairs)  16.2 us
    ppermute x6, starting transfers between devices, up(): return lax.ppermute(value, 'row', pairs)  14.5 us
    ppermute x6, starting transfers between devices, exchange(): lax.ppermute(term, 'row', [(i, i ^ distance) for i in range(8)])  10.8 us
    ppermute x6, starting transfers between devices, down(): return lax.ppermute(value, 'row', pairs)  7.71 us
  transfers between devices with their start and end apart: 29, of which 16 were waited for; matrix products, arithmetic and copies ran while one was open for 4% of the time, Pallas kernels for 39%

profile of v2, /device:TPU:0, one launch (start us, length us, event | category | flops | bytes accessed | tf_op | source)
XLA Modules:
  0.0 282.8 jit_solution(13643945009632678432)
XLA Ops:
  2.2 3.9 %prepare.1 = (f32[512,768]{1,0:T(8,128)}, f32[512,256]{1,0:T(8,128)}) custom-call(s32[1]{0:T(128)} %bitcast.me_ref, s32[64,2]{1,0:T(8,128)} %copy.10.pattern_ref, f32[2,1,512,512]{3,2,1,0:T(8,128)} %panel_ref.1), custom_call_target="tpu_custom_call" | custom-call | tf_op jit(solution)/shard_map/prepare/pallas_call | solution.py:103
  10.2 4.6 %collective-permute-start.1 = (f32[512,768]{1,0:T(8,128)}, f32[512,768]{1,0:T(8,128)}, u32[]{:S(2)}, u32[]{:S(2)}) collective-permute-start(f32[512,768]{1,0:T(8,128)} %get-tuple-element.84.refs_0_), channel_id=1, source_target_pairs={{0,4},{2,6},{4,8},{6,10},{8,12},{10,14},{1,5},{3,7},{5,9},{7,11},{... | collective-permute-start | bytes 4718600 | tf_op jit(solution)/shard_map/ppermute | solution.py:306
  22.3 2.8 copy.12
  26.9 29.9 %collective-permute-done.4 = f32[512,256]{1,0:T(8,128)} collective-permute-done((f32[512,256]{1,0:T(8,128)S(1)}, f32[512,256]{1,0:T(8,128)}, u32[]{:S(2)}, u32[]{:S(2)}) %collective-permute-start.4) | collective-permute-done | bytes 524320 | tf_op jit(solution)/shard_map/ppermute | solution.py:314
  56.8 3.7 %collective-permute-start.7 = (f32[512,768]{1,0:T(8,128)}, f32[512,768]{1,0:T(8,128)}, u32[]{:S(2)}, u32[]{:S(2)}) collective-permute-start(f32[512,768]{1,0:T(8,128)} %collective-permute-done.refs_2_), channel_id=1, source_target_pairs={{0,2},{2,0},{1,3},{3,1},{16,18},{18,16},{17,19},{19,17}} | collective-permute-start | bytes 4718600 | tf_op jit(solution)/shard_map/ppermute | solution.py:314
  67.5 17.3 %slots_768_1.4.refs_4_ = f32[1024,768]{1,0:T(8,128)} custom-call(s32[10]{0:T(128)} %stack.61.table_ref, f32[2,1,1024,4096]{3,2,1,0:T(8,128)} %a_ref.13, f32[512,768]{1,0:T(8,128)} %get-tuple-element.84.refs_0_, f32[512,768]{1,0:T(8,128)} %collective-permute-done.2.refs_1_), custom_call_target="tpu_custom_call" | custom-call | flops 4831838208 | bytes 4194304 | tf_op jit(solution)/shard_map/slots_768_1/pallas_call | solution.py:215
  84.8 10.5 %collective-permute-done.7.refs_3_ = f32[512,768]{1,0:T(8,128)} collective-permute-done((f32[512,768]{1,0:T(8,128)}, f32[512,768]{1,0:T(8,128)}, u32[]{:S(2)}, u32[]{:S(2)}) %collective-permute-start.7) | collective-permute-done | bytes 1572896 | tf_op jit(solution)/shard_map/ppermute | solution.py:314
  95.3 3.2 %collective-permute-done.5.refs_4_ = f32[512,768]{1,0:T(8,128)} collective-permute-done((f32[512,768]{1,0:T(8,128)}, f32[512,768]{1,0:T(8,128)}, u32[]{:S(2)}, u32[]{:S(2)}) %collective-permute-start.5) | collective-permute-done | bytes 1572896 | tf_op jit(solution)/shard_map/ppermute | solution.py:310
  107.7 9.3 %slots_256_1.2.refs_10_ = f32[1024,256]{1,0:T(8,128)} custom-call(s32[10]{0:T(128)} %stack.61.table_ref, f32[2,1,1024,4096]{3,2,1,0:T(8,128)} %a_ref.13, f32[1024,256]{1,0:T(8,128)} %pad_maximum_fusion.2.refs_0_.refs_1_, f32[1024,256]{1,0:T(8,128)} %pad_maximum_fusion.2.refs_0_.refs_1_), custom_call_target="tpu_custom_call" | custom-call | flops 1610612736 | bytes 4194304 | tf_op jit(solution)/shard_map/slots_256_1/pallas_call | solution.py:215
  117.0 18.2 %slots_768_1.5.refs_6_ = f32[1024,768]{1,0:T(8,128)} custom-call(s32[10]{0:T(128)} %stack.61.table_ref, f32[2,1,1024,4096]{3,2,1,0:T(8,128)} %a_ref.13, f32[512,768]{1,0:T(8,128)} %collective-permute-done.1.refs_0_, f32[512,768]{1,0:T(8,128)} %collective-permute-done.8.refs_1_, f32[512,768]{1,0:T(8,128)} %collective-permute-done.refs_2_, ...), custom_call_target="tpu_custom_call" | custom-call | flops 4831838208 | bytes 4194304 | tf_op jit(solution)/shard_map/slots_768_1/pallas_call | solution.py:215
  137.3 5.3 %collective-permute-done.9 = f32[512,768]{1,0:T(8,128)} collective-permute-done((f32[512,768]{1,0:T(8,128)}, f32[512,768]{1,0:T(8,128)}, u32[]{:S(2)}, u32[]{:S(2)}) %collective-permute-start.9) | collective-permute-done | bytes 1572896 | tf_op jit(solution)/shard_map/ppermute | solution.py:310
  142.6 3.0 %select_select_fusion.refs_0_ = f32[512,768]{1,0:T(8,128)} fusion(f32[512,768]{1,0:T(8,128)} %collective-permute-done.5.refs_4_, f32[512,768]{1,0:T(8,128)} %collective-permute-done.10, f32[512,768]{1,0:T(8,128)} %collective-permute-done.6.refs_0_, f32[512,768]{1,0:T(8,128)} %collective-permute-done.9, pred[]{:T(512)S(6)} %eq.15, pred[]{:T(512)S(6)} %eq.16, ...), kind=kLoop, calls=%fused_computation.3 | loop fusion | flops 1179648 | bytes 7864323 | tf_op jit(solution)/shard_map/jit(_where)/select_n | solution.py:351
  147.1 2.9 %collective-permute-start.16 = (f32[1024,256]{1,0:T(8,128)}, f32[1024,256]{1,0:T(8,128)}, u32[]{:S(2)}, u32[]{:S(2)}) collective-permute-start(f32[1024,256]{1,0:T(8,128)} %pad_maximum_fusion.2.refs_0_.refs_1_), channel_id=1, source_target_pairs={{0,4},{2,6},{4,8},{6,10},{8,12},{10,14},{1,5},{3,7},{5,9},{7,11},{... | collective-permute-start | bytes 3145736 | tf_op jit(solution)/shard_map/ppermute | solution.py:306
  151.2 18.2 %slots_768_1.6.refs_2_ = f32[1024,768]{1,0:T(8,128)} custom-call(s32[10]{0:T(128)} %stack.61.table_ref, f32[2,1,1024,4096]{3,2,1,0:T(8,128)} %a_ref.13, f32[512,768]{1,0:T(8,128)} %collective-permute-done.6.refs_0_, f32[512,768]{1,0:T(8,128)} %collective-permute-done.13.refs_1_, f32[512,768]{1,0:T(8,128)} %collective-permute-done.refs_2_, ...), custom_call_target="tpu_custom_call" | custom-call | flops 4831838208 | bytes 4194304 | tf_op jit(solution)/shard_map/slots_768_1/pallas_call | solution.py:215
  169.6 8.3 %collective-permute-done.15.refs_2_.refs_3_.refs_6_.refs_7_ = f32[1024,256]{1,0:T(8,128)} collective-permute-done((f32[1024,256]{1,0:T(8,128)}, f32[1024,256]{1,0:T(8,128)}, u32[]{:S(2)}, u32[]{:S(2)}) %collective-permute-start.15) | collective-permute-done | bytes 1048608 | tf_op jit(solution)/shard_map/ppermute | solution.py:310
  182.4 18.4 %slots_768_1.7 = (f32[1024,384]{1,0:T(8,128)}, f32[1024,384]{1,0:T(8,128)}) custom-call(s32[10]{0:T(128)} %stack.61.table_ref, f32[2,1,1024,4096]{3,2,1,0:T(8,128)} %a_ref.13, f32[512,768]{1,0:T(8,128)} %select_select_fusion.refs_0_, f32[512,768]{1,0:T(8,128)} %collective-permute-done.14.refs_1_, f32[1024,768]{1,0:T(8,128)} %slots_768_1.6.refs_2_), custom_call_target="tpu_custom_call" | custom-call | flops 4831838208 | bytes 4194304 | tf_op jit(solution)/shard_map/slots_768_1/pallas_call | solution.py:215
  214.2 14.2 %slots_256_2.1.refs_8_ = f32[1024,256]{1,0:T(8,128)} custom-call(s32[10]{0:T(128)} %stack.61.table_ref, f32[2,1,1024,4096]{3,2,1,0:T(8,128)} %a_ref.13, f32[1024,256]{1,0:T(8,128)} %collective-permute-done.16.refs_0_.refs_1_, f32[1024,256]{1,0:T(8,128)} %collective-permute-done.16.refs_0_.refs_1_, ...), custom_call_target="tpu_custom_call" | custom-call | flops 3221225472 | bytes 8388608 | tf_op jit(solution)/shard_map/slots_256_2/pallas_call | solution.py:215
  228.5 6.5 %collective-permute-done.19.refs_6_.refs_7_ = f32[1024,256]{1,0:T(8,128)} collective-permute-done((f32[1024,256]{1,0:T(8,128)}, f32[1024,256]{1,0:T(8,128)}, u32[]{:S(2)}, u32[]{:S(2)}) %collective-permute-start.19) | collective-permute-done | bytes 1048608 | tf_op jit(solution)/shard_map/ppermute | solution.py:310
  235.4 9.7 %slots_256_1.3 = (f32[1024,128]{1,0:T(8,128)}, f32[1024,128]{1,0:T(8,128)}) custom-call(s32[10]{0:T(128)} %stack.61.table_ref, f32[2,1,1024,4096]{3,2,1,0:T(8,128)} %a_ref.13, f32[1024,256]{1,0:T(8,128)} %collective-permute-done.18.refs_4_.refs_5_.refs_0_.refs_1_, f32[1024,256]{1,0:T(8,128)} %collective-permute-done.18.refs_4_.refs_5_.refs_0_.refs_1_, ...), custom_call_target="tpu_custom_call" | custom-call | flops 1610612736 | bytes 4194304 | tf_op jit(solution)/shard_map/slots_256_1/pallas_call | solution.py:215
  246.1 7.0 %collective-permute-start.25 = (f32[256,384]{1,0:T(8,128)S(1)}, f32[256,384]{1,0:T(8,128)S(1)}, u32[]{:S(2)}, u32[]{:S(2)}) collective-permute-start(f32[256,384]{1,0:T(8,128)S(1)} %add.29), channel_id=1, source_target_pairs={{0,8},{2,10},{4,12},{6,14},{8,0},{10,2},{12,4},{14,6},{1,9},{3,11}... | collective-permute-start | bytes 1179656 | tf_op jit(solution)/shard_map/ppermute | solution.py:393
  257.5 2.7 assemble.1
  261.9 8.8 %collective-permute-done.25 = f32[256,384]{1,0:T(8,128)S(1)} collective-permute-done((f32[256,384]{1,0:T(8,128)S(1)}, f32[256,384]{1,0:T(8,128)S(1)}, u32[]{:S(2)}, u32[]{:S(2)}) %collective-permute-start.25) | collective-permute-done | bytes 393248 | tf_op jit(solution)/shard_map/ppermute | solution.py:393
  270.9 2.5 collective-permute-done.27
  273.6 8.1 %collective-permute-done.28 = f32[256,128]{1,0:T(8,128)S(1)} collective-permute-done((f32[256,128]{1,0:T(8,128)S(1)}, f32[256,128]{1,0:T(8,128)S(1)}, u32[]{:S(2)}, u32[]{:S(2)}) %collective-permute-start.28) | collective-permute-done | bytes 131104 | tf_op jit(solution)/shard_map/ppermute | solution.py:393
  (89 shorter events, 63.0 us)
Async XLA Ops:
  7.2 11.8 %collective-permute-start.3 = (f32[2,512,256]{2,1,0:T(8,128)}, f32[2,512,256]{2,1,0:T(8,128)}, u32[]{:S(2)}, u32[]{:S(2)}) collective-permute-start(f32[2,512,256]{2,1,0:T(8,128)} %slice_select_fusion), channel_id=1, source_target_pairs={{0,1},{1,0},{2,3},{3,2},{4,5},{5,4},{6,7},{7,6},{8,9},{9,8},{10,11... | collective-permute-start | bytes 3145736 | tf_op jit(solution)/shard_map/ppermute | solution.py:317
  7.7 49.1 %collective-permute-start.2 = (f32[512,768]{1,0:T(8,128)}, f32[512,768]{1,0:T(8,128)}, u32[]{:S(2)}, u32[]{:S(2)}) collective-permute-start(f32[512,768]{1,0:T(8,128)} %get-tuple-element.84.refs_0_), channel_id=1, source_target_pairs={{0,2},{2,0},{4,6},{6,4},{8,10},{10,8},{12,14},{14,12},{1,3},{3,1},... | collective-permute-start | bytes 4718600 | tf_op jit(solution)/shard_map/ppermute | solution.py:314
  10.2 46.6 %collective-permute-start.1 = (f32[512,768]{1,0:T(8,128)}, f32[512,768]{1,0:T(8,128)}, u32[]{:S(2)}, u32[]{:S(2)}) collective-permute-start(f32[512,768]{1,0:T(8,128)} %get-tuple-element.84.refs_0_), channel_id=1, source_target_pairs={{0,4},{2,6},{4,8},{6,10},{8,12},{10,14},{1,5},{3,7},{5,9},{7,11},{... | collective-permute-start | bytes 4718600 | tf_op jit(solution)/shard_map/ppermute | solution.py:306
  14.8 42.0 %collective-permute-start = (f32[512,768]{1,0:T(8,128)}, f32[512,768]{1,0:T(8,128)}, u32[]{:S(2)}, u32[]{:S(2)}) collective-permute-start(f32[512,768]{1,0:T(8,128)} %get-tuple-element.84.refs_0_), channel_id=1, source_target_pairs={{4,0},{6,2},{8,4},{10,6},{12,8},{14,10},{5,1},{7,3},{9,5},{11,7},{... | collective-permute-start | bytes 4718600 | tf_op jit(solution)/shard_map/ppermute | solution.py:310
  16.1 40.7 %collective-permute-start.4 = (f32[512,256]{1,0:T(8,128)S(1)}, f32[512,256]{1,0:T(8,128)}, u32[]{:S(2)}, u32[]{:S(2)}) collective-permute-start(f32[512,256]{1,0:T(8,128)S(1)} %copy-done.7), channel_id=1, source_target_pairs={{0,2},{2,0},{4,6},{6,4},{8,10},{10,8},{12,14},{14,12},{1,3},{3,1},... | collective-permute-start | bytes 1572872 | tf_op jit(solution)/shard_map/ppermute | solution.py:314
  56.8 38.4 %collective-permute-start.7 = (f32[512,768]{1,0:T(8,128)}, f32[512,768]{1,0:T(8,128)}, u32[]{:S(2)}, u32[]{:S(2)}) collective-permute-start(f32[512,768]{1,0:T(8,128)} %collective-permute-done.refs_2_), channel_id=1, source_target_pairs={{0,2},{2,0},{1,3},{3,1},{16,18},{18,16},{17,19},{19,17}} | collective-permute-start | bytes 4718600 | tf_op jit(solution)/shard_map/ppermute | solution.py:314
  60.5 38.0 %collective-permute-start.5 = (f32[512,768]{1,0:T(8,128)}, f32[512,768]{1,0:T(8,128)}, u32[]{:S(2)}, u32[]{:S(2)}) collective-permute-start(f32[512,768]{1,0:T(8,128)} %collective-permute-done.refs_2_), channel_id=1, source_target_pairs={{4,0},{6,2},{8,4},{10,6},{5,1},{7,3},{9,5},{11,7},{20,16},{22,18},... | collective-permute-start | bytes 4718600 | tf_op jit(solution)/shard_map/ppermute | solution.py:310
  61.8 36.7 %collective-permute-start.8 = (f32[512,768]{1,0:T(8,128)}, f32[512,768]{1,0:T(8,128)}, u32[]{:S(2)}, u32[]{:S(2)}) collective-permute-start(f32[512,768]{1,0:T(8,128)} %collective-permute-done.1.refs_0_), channel_id=1, source_target_pairs={{4,6},{6,4},{8,10},{10,8},{12,14},{14,12},{5,7},{7,5},{9,11},{11,9... | collective-permute-start | bytes 4718600 | tf_op jit(solution)/shard_map/ppermute | solution.py:314
  63.7 34.8 %collective-permute-start.6 = (f32[512,768]{1,0:T(8,128)}, f32[512,768]{1,0:T(8,128)}, u32[]{:S(2)}, u32[]{:S(2)}) collective-permute-start(f32[512,768]{1,0:T(8,128)} %collective-permute-done.1.refs_0_), channel_id=1, source_target_pairs={{4,8},{6,10},{8,12},{10,14},{5,9},{7,11},{9,13},{11,15},{20,24},{2... | collective-permute-start | bytes 4718600 | tf_op jit(solution)/shard_map/ppermute | solution.py:306
  98.5 36.7 %collective-permute-start.11 = (f32[512,768]{1,0:T(8,128)}, f32[512,768]{1,0:T(8,128)}, u32[]{:S(2)}, u32[]{:S(2)}) collective-permute-start(f32[512,768]{1,0:T(8,128)} %collective-permute-done.refs_2_), channel_id=1, source_target_pairs={{4,6},{6,4},{8,10},{10,8},{5,7},{7,5},{9,11},{11,9},{20,22},{22,20... | collective-permute-start | bytes 4718600 | tf_op jit(solution)/shard_map/ppermute | solution.py:314
  100.3 37.0 %collective-permute-start.12 = (f32[512,768]{1,0:T(8,128)}, f32[512,768]{1,0:T(8,128)}, u32[]{:S(2)}, u32[]{:S(2)}) collective-permute-start(f32[512,768]{1,0:T(8,128)} %collective-permute-done.5.refs_4_), channel_id=1, source_target_pairs={{0,2},{2,0},{1,3},{3,1},{16,18},{18,16},{17,19},{19,17}} | collective-permute-start | bytes 4718600 | tf_op jit(solution)/shard_map/ppermute | solution.py:314
  102.7 39.9 %collective-permute-start.9 = (f32[512,768]{1,0:T(8,128)}, f32[512,768]{1,0:T(8,128)}, u32[]{:S(2)}, u32[]{:S(2)}) collective-permute-start(f32[512,768]{1,0:T(8,128)} %collective-permute-done.5.refs_4_), channel_id=1, source_target_pairs={{4,0},{6,2},{5,1},{7,3},{20,16},{22,18},{21,17},{23,19}} | collective-permute-start | bytes 4718600 | tf_op jit(solution)/shard_map/ppermute | solution.py:310
  104.0 38.6 %collective-permute-start.13 = (f32[512,768]{1,0:T(8,128)}, f32[512,768]{1,0:T(8,128)}, u32[]{:S(2)}, u32[]{:S(2)}) collective-permute-start(f32[512,768]{1,0:T(8,128)} %collective-permute-done.6.refs_0_), channel_id=1, source_target_pairs={{12,14},{14,12},{13,15},{15,13},{28,30},{30,28},{29,31},{31,29}} | collective-permute-start | bytes 4718600 | tf_op jit(solution)/shard_map/ppermute | solution.py:314
  105.8 36.8 %collective-permute-start.10 = (f32[512,768]{1,0:T(8,128)}, f32[512,768]{1,0:T(8,128)}, u32[]{:S(2)}, u32[]{:S(2)}) collective-permute-start(f32[512,768]{1,0:T(8,128)} %collective-permute-done.6.refs_0_), channel_id=1, source_target_pairs={{8,12},{10,14},{9,13},{11,15},{24,28},{26,30},{25,29},{27,31}} | collective-permute-start | bytes 4718600 | tf_op jit(solution)/shard_map/ppermute | solution.py:306
  145.5 33.9 %collective-permute-start.14 = (f32[512,768]{1,0:T(8,128)}, f32[512,768]{1,0:T(8,128)}, u32[]{:S(2)}, u32[]{:S(2)}) collective-permute-start(f32[512,768]{1,0:T(8,128)} %select_select_fusion.refs_0_), channel_id=1, source_target_pairs={{0,2},{2,0},{4,6},{6,4},{8,10},{10,8},{12,14},{14,12},{1,3},{3,1},... | collective-permute-start | bytes 4718600 | tf_op jit(solution)/shard_map/ppermute | solution.py:314
  147.1 22.5 %collective-permute-start.16 = (f32[1024,256]{1,0:T(8,128)}, f32[1024,256]{1,0:T(8,128)}, u32[]{:S(2)}, u32[]{:S(2)}) collective-permute-start(f32[1024,256]{1,0:T(8,128)} %pad_maximum_fusion.2.refs_0_.refs_1_), channel_id=1, source_target_pairs={{0,4},{2,6},{4,8},{6,10},{8,12},{10,14},{1,5},{3,7},{5,9},{7,11},{... | collective-permute-start | bytes 3145736 | tf_op jit(solution)/shard_map/ppermute | solution.py:306
  150.0 27.9 %collective-permute-start.15 = (f32[1024,256]{1,0:T(8,128)}, f32[1024,256]{1,0:T(8,128)}, u32[]{:S(2)}, u32[]{:S(2)}) collective-permute-start(f32[1024,256]{1,0:T(8,128)} %pad_maximum_fusion.2.refs_0_.refs_1_), channel_id=1, source_target_pairs={{4,0},{6,2},{8,4},{10,6},{12,8},{14,10},{5,1},{7,3},{9,5},{11,7},{... | collective-permute-start | bytes 3145736 | tf_op jit(solution)/shard_map/ppermute | solution.py:310
  179.5 23.7 %collective-permute-start.17 = (f32[1024,256]{1,0:T(8,128)}, f32[1024,256]{1,0:T(8,128)}, u32[]{:S(2)}, u32[]{:S(2)}) collective-permute-start(f32[1024,256]{1,0:T(8,128)} %collective-permute-done.15.refs_2_.refs_3_.refs_6_.refs_7_), channel_id=1, source_target_pairs={{4,0},{6,2},{8,4},{10,6},{5,1},{7,3},{9,5},{11,7},{20,16},{22,18},... | collective-permute-start | bytes 3145736 | tf_op jit(solution)/shard_map/ppermute | solution.py:310
  180.8 22.4 %collective-permute-start.18 = (f32[1024,256]{1,0:T(8,128)}, f32[1024,256]{1,0:T(8,128)}, u32[]{:S(2)}, u32[]{:S(2)}) collective-permute-start(f32[1024,256]{1,0:T(8,128)} %collective-permute-done.16.refs_0_.refs_1_), channel_id=1, source_target_pairs={{4,8},{6,10},{8,12},{10,14},{5,9},{7,11},{9,13},{11,15},{20,24},{2... | collective-permute-start | bytes 3145736 | tf_op jit(solution)/shard_map/ppermute | solution.py:306
  203.2 31.9 %collective-permute-start.19 = (f32[1024,256]{1,0:T(8,128)}, f32[1024,256]{1,0:T(8,128)}, u32[]{:S(2)}, u32[]{:S(2)}) collective-permute-start(f32[1024,256]{1,0:T(8,128)} %collective-permute-done.17.refs_8_.refs_9_.refs_4_.refs_5_), channel_id=1, source_target_pairs={{4,0},{6,2},{5,1},{7,3},{20,16},{22,18},{21,17},{23,19}} | collective-permute-start | bytes 3145736 | tf_op jit(solution)/shard_map/ppermute | solution.py:310
  204.4 30.6 %collective-permute-start.20 = (f32[1024,256]{1,0:T(8,128)}, f32[1024,256]{1,0:T(8,128)}, u32[]{:S(2)}, u32[]{:S(2)}) collective-permute-start(f32[1024,256]{1,0:T(8,128)} %collective-permute-done.18.refs_4_.refs_5_.refs_0_.refs_1_), channel_id=1, source_target_pairs={{8,12},{10,14},{9,13},{11,15},{24,28},{26,30},{25,29},{27,31}} | collective-permute-start | bytes 3145736 | tf_op jit(solution)/shard_map/ppermute | solution.py:306
  212.7 15.8 %collective-permute-start.22 = (f32[256,384]{1,0:T(8,128)S(1)}, f32[256,384]{1,0:T(8,128)S(1)}, u32[]{:S(2)}, u32[]{:S(2)}) collective-permute-start(f32[256,384]{1,0:T(8,128)S(1)} %get-tuple-element.144), channel_id=1, source_target_pairs={{0,2},{2,0},{4,6},{6,4},{8,10},{10,8},{12,14},{14,12},{1,3},{3,1},... | collective-permute-start | bytes 1179656 | tf_op jit(solution)/shard_map/ppermute | solution.py:393
  246.1 24.7 %collective-permute-start.25 = (f32[256,384]{1,0:T(8,128)S(1)}, f32[256,384]{1,0:T(8,128)S(1)}, u32[]{:S(2)}, u32[]{:S(2)}) collective-permute-start(f32[256,384]{1,0:T(8,128)S(1)} %add.29), channel_id=1, source_target_pairs={{0,8},{2,10},{4,12},{6,14},{8,0},{10,2},{12,4},{14,6},{1,9},{3,11}... | collective-permute-start | bytes 1179656 | tf_op jit(solution)/shard_map/ppermute | solution.py:393
  261.6 11.9 %collective-permute-start.27 = (f32[256,128]{1,0:T(8,128)S(1)}, f32[256,128]{1,0:T(8,128)S(1)}, u32[]{:S(2)}, u32[]{:S(2)}) collective-permute-start(f32[256,128]{1,0:T(8,128)S(1)} %add.31), channel_id=1, source_target_pairs={{0,4},{2,6},{4,0},{6,2},{8,12},{10,14},{12,8},{14,10},{1,5},{3,7},... | collective-permute-start | bytes 393224 | tf_op jit(solution)/shard_map/ppermute | solution.py:393
  (14 other events, 79.9 us)

commit v3 on v2

--- a/solution.py
+++ b/solution.py
@@ -353,9 +353,9 @@
 
     def cross(chain, slot):
         names, _, choices = layout[slot]
-        if slot == 3:
+        if slot in (1, 3):
             select(chain, slot)
-        if slot in (0, 3):
+        if slot != 2:
             live[f"{chain} y{slot}"] = across(live[f"{chain} {slot}"])
             return
         for j, name in enumerate(names):
@@ -367,7 +367,7 @@
         for k in wanted:
             if chain == "t":
                 slots.append([(live[f"t {name}"],) * 2 for name in layout[k][0]])
-            elif k in (1, 2):
+            elif k == 2:
                 slots.append([(live[f"{chain} {name}"], live[f"{chain} y{k} {name}"]) for name in layout[k][0]])
             else:
                 slots.append([(live[f"{chain} {k}"], live[f"{chain} y{k}"])])
@@ -422,7 +422,7 @@
     fence()
     mine, theirs = add("t", (3,), last=True)
     update_last, term_last = finish(mine, swap(theirs), live["mask"], live["lower"])
-    live["term c"] = exchange(exchange(live["term c"], 2), 4)
+    live["term c"] = exchange(exchange(live["term c"], 4), 2)
     for distance in (1, 2, 4):
         term_last = exchange(term_last, distance)
 

time: 284 us -> 279 us (0.982)
  waiting for transfers between devices: 92.3 us -> 85.5 us
    ppermute x6, waiting for transfers between devices: 21.6 us -> 16.5 us  [exchange(): lax.ppermute(term, 'row', [(i, i ^ distance) for i in range(8)])]
    ppermute x6, waiting for transfers between devices: 25.6 us -> 21.9 us  [down(): return lax.ppermute(value, 'row', pairs)]
    ppermute x8 -> x7, starting transfers between devices: 16.2 us -> 12.5 us  [across(): return lax.ppermute(value, 'row', pairs)]
    select_n x1 -> x2, other arithmetic: 2.96 us -> 5.71 us  [select(): value = jnp.where(chosen, live[f'{chain} {name}'], value)]
    ppermute x8 -> x7, waiting for transfers between devices: 44.2 us -> 46.3 us  [across(): return lax.ppermute(value, 'row', pairs)]
  transfers between devices with their start and end apart: 29 -> 28, of which waited for: 16 -> 16; matrix products, arithmetic and copies ran while one was open for 4% -> 5% of each run, Pallas kernels for 39% -> 40%
where the time goes in v3:
time: 279 us; the launch traced here: 278 us
  Pallas kernels  115 us (41%)
  waiting for transfers between devices  85.5 us (31%)
  starting transfers between devices  47.7 us (17%)
  local copies, waits for them, and re-layouts  15 us (5%)
  other arithmetic  14.3 us (5%)
    pallas_call x7, Pallas kernels, add_slots(): pl.pallas_call(functools.partial(slots_kernel, wanted=wanted, counts=coun...  105 us
    ppermute x7, waiting for transfers between devices, across(): return lax.ppermute(value, 'row', pairs)  46.3 us
    ppermute x6, waiting for transfers between devices, down(): return lax.ppermute(value, 'row', pairs)  21.9 us
    ppermute x6, waiting for transfers between devices, exchange(): lax.ppermute(term, 'row', [(i, i ^ distance) for i in range(8)])  16.5 us
    ppermute x6, starting transfers between devices, up(): return lax.ppermute(value, 'row', pairs)  14.5 us
    ppermute x7, starting transfers between devices, across(): return lax.ppermute(value, 'row', pairs)  12.5 us
    ppermute x6, starting transfers between devices, exchange(): lax.ppermute(term, 'row', [(i, i ^ distance) for i in range(8)])  12.4 us
    ppermute x6, starting transfers between devices, down(): return lax.ppermute(value, 'row', pairs)  7.69 us
  transfers between devices with their start and end apart: 28, of which 16 were waited for; matrix products, arithmetic and copies ran while one was open for 5% of the time, Pallas kernels for 40%

profile of v3, /device:TPU:0, one launch (start us, length us, event | category | flops | bytes accessed | tf_op | source)
XLA Modules:
  0.0 278.2 jit_solution(3083939834957063742)
XLA Ops:
  2.2 3.9 %prepare.1 = (f32[512,768]{1,0:T(8,128)}, f32[512,256]{1,0:T(8,128)}) custom-call(s32[1]{0:T(128)} %bitcast.me_ref, s32[64,2]{1,0:T(8,128)} %copy.10.pattern_ref, f32[2,1,512,512]{3,2,1,0:T(8,128)} %panel_ref.1), custom_call_target="tpu_custom_call" | custom-call | tf_op jit(solution)/shard_map/prepare/pallas_call | solution.py:103
  10.2 4.6 %collective-permute-start.1 = (f32[512,768]{1,0:T(8,128)}, f32[512,768]{1,0:T(8,128)}, u32[]{:S(2)}, u32[]{:S(2)}) collective-permute-start(f32[512,768]{1,0:T(8,128)} %get-tuple-element.83.refs_0_), channel_id=1, source_target_pairs={{0,4},{2,6},{4,8},{6,10},{8,12},{10,14},{1,5},{3,7},{5,9},{7,11},{... | collective-permute-start | bytes 4718600 | tf_op jit(solution)/shard_map/ppermute | solution.py:306
  20.5 2.9 %copy.11 = f32[2,512,2,256]{3,0,2,1:T(2,128)} copy(f32[2,512,2,256]{3,1,0,2:T(8,128)S(1)} %pad_maximum_fusion) | data formatting | bytes 4194304 | tf_op jit(solution)/shard_map/stack | solution.py:389
  23.4 4.2 %copy.12 = f32[2,1024,256]{1,2,0:T(8,128)} copy(f32[2,1024,256]{2,0,1:T(2,128)} %bitcast.38) | data formatting | bytes 4194304 | tf_op jit(solution)/shard_map/reshape | solution.py:389
  29.6 27.2 %collective-permute-done.4 = f32[512,256]{1,0:T(8,128)} collective-permute-done((f32[512,256]{1,0:T(8,128)}, f32[512,256]{1,0:T(8,128)}, u32[]{:S(2)}, u32[]{:S(2)}) %collective-permute-start.4) | collective-permute-done | bytes 524320 | tf_op jit(solution)/shard_map/ppermute | solution.py:314
  66.7 17.3 %slots_768_1.4.refs_2_ = f32[1024,768]{1,0:T(8,128)} custom-call(s32[10]{0:T(128)} %stack.61.table_ref, f32[2,1,1024,4096]{3,2,1,0:T(8,128)} %a_ref.13, f32[512,768]{1,0:T(8,128)} %get-tuple-element.83.refs_0_, f32[512,768]{1,0:T(8,128)} %collective-permute-done.2.refs_1_), custom_call_target="tpu_custom_call" | custom-call | flops 4831838208 | bytes 4194304 | tf_op jit(solution)/shard_map/slots_768_1/pallas_call | solution.py:215
  84.0 12.1 %collective-permute-done.7.refs_1_ = f32[512,768]{1,0:T(8,128)} collective-permute-done((f32[512,768]{1,0:T(8,128)}, f32[512,768]{1,0:T(8,128)}, u32[]{:S(2)}, u32[]{:S(2)}) %collective-permute-start.7) | collective-permute-done | bytes 1572896 | tf_op jit(solution)/shard_map/ppermute | solution.py:314
  96.1 7.3 %collective-permute-done.5.refs_4_ = f32[512,768]{1,0:T(8,128)} collective-permute-done((f32[512,768]{1,0:T(8,128)}, f32[512,768]{1,0:T(8,128)}, u32[]{:S(2)}, u32[]{:S(2)}) %collective-permute-start.5) | collective-permute-done | bytes 1572896 | tf_op jit(solution)/shard_map/ppermute | solution.py:310
  112.8 9.3 %slots_256_1.2.refs_10_ = f32[1024,256]{1,0:T(8,128)} custom-call(s32[10]{0:T(128)} %stack.61.table_ref, f32[2,1,1024,4096]{3,2,1,0:T(8,128)} %a_ref.13, f32[1024,256]{1,0:T(8,128)} %pad_maximum_fusion.2.refs_0_.refs_1_, f32[1024,256]{1,0:T(8,128)} %pad_maximum_fusion.2.refs_0_.refs_1_), custom_call_target="tpu_custom_call" | custom-call | flops 1610612736 | bytes 4194304 | tf_op jit(solution)/shard_map/slots_256_1/pallas_call | solution.py:215
  122.1 18.2 %slots_768_1.5.refs_6_ = f32[1024,768]{1,0:T(8,128)} custom-call(s32[10]{0:T(128)} %stack.61.table_ref, f32[2,1,1024,4096]{3,2,1,0:T(8,128)} %a_ref.13, f32[512,768]{1,0:T(8,128)} %broadcast_select_fusion.refs_0_, f32[512,768]{1,0:T(8,128)} %collective-permute-done.7.refs_1_, f32[1024,768]{1,0:T(8,128)} %slots_768_1.4.refs_2_), custom_call_target="tpu_custom_call" | custom-call | flops 4831838208 | bytes 4194304 | tf_op jit(solution)/shard_map/slots_768_1/pallas_call | solution.py:215
  144.5 3.0 %select_select_fusion.refs_0_ = f32[512,768]{1,0:T(8,128)} fusion(f32[512,768]{1,0:T(8,128)} %collective-permute-done.5.refs_4_, f32[512,768]{1,0:T(8,128)} %collective-permute-done.9, f32[512,768]{1,0:T(8,128)} %collective-permute-done.6.refs_0_, f32[512,768]{1,0:T(8,128)} %collective-permute-done.8, pred[]{:T(512)S(6)} %eq.15, pred[]{:T(512)S(6)} %eq.16, ...), kind=kLoop, calls=%fused_computation.3 | loop fusion | flops 1179648 | bytes 7864323 | tf_op jit(solution)/shard_map/jit(_where)/select_n | solution.py:351
  149.0 2.9 %collective-permute-start.15 = (f32[1024,256]{1,0:T(8,128)}, f32[1024,256]{1,0:T(8,128)}, u32[]{:S(2)}, u32[]{:S(2)}) collective-permute-start(f32[1024,256]{1,0:T(8,128)} %pad_maximum_fusion.2.refs_0_.refs_1_), channel_id=1, source_target_pairs={{0,4},{2,6},{4,8},{6,10},{8,12},{10,14},{1,5},{3,7},{5,9},{7,11},{... | collective-permute-start | bytes 3145736 | tf_op jit(solution)/shard_map/ppermute | solution.py:306
  153.2 18.2 %slots_768_1.6.refs_2_ = f32[1024,768]{1,0:T(8,128)} custom-call(s32[10]{0:T(128)} %stack.61.table_ref, f32[2,1,1024,4096]{3,2,1,0:T(8,128)} %a_ref.13, f32[512,768]{1,0:T(8,128)} %collective-permute-done.6.refs_0_, f32[512,768]{1,0:T(8,128)} %collective-permute-done.12.refs_1_, f32[512,768]{1,0:T(8,128)} %collective-permute-done.refs_2_, ...), custom_call_target="tpu_custom_call" | custom-call | flops 4831838208 | bytes 4194304 | tf_op jit(solution)/shard_map/slots_768_1/pallas_call | solution.py:215
  171.5 5.1 %collective-permute-done.14.refs_2_.refs_3_.refs_6_.refs_7_ = f32[1024,256]{1,0:T(8,128)} collective-permute-done((f32[1024,256]{1,0:T(8,128)}, f32[1024,256]{1,0:T(8,128)}, u32[]{:S(2)}, u32[]{:S(2)}) %collective-permute-start.14) | collective-permute-done | bytes 1048608 | tf_op jit(solution)/shard_map/ppermute | solution.py:310
  176.6 4.8 %collective-permute-done.13.refs_1_ = f32[512,768]{1,0:T(8,128)} collective-permute-done((f32[512,768]{1,0:T(8,128)}, f32[512,768]{1,0:T(8,128)}, u32[]{:S(2)}, u32[]{:S(2)}) %collective-permute-start.13) | collective-permute-done | bytes 1572896 | tf_op jit(solution)/shard_map/ppermute | solution.py:314
  184.4 18.3 %slots_768_1.7 = (f32[1024,384]{1,0:T(8,128)}, f32[1024,384]{1,0:T(8,128)}) custom-call(s32[10]{0:T(128)} %stack.61.table_ref, f32[2,1,1024,4096]{3,2,1,0:T(8,128)} %a_ref.13, f32[512,768]{1,0:T(8,128)} %select_select_fusion.refs_0_, f32[512,768]{1,0:T(8,128)} %collective-permute-done.13.refs_1_, f32[1024,768]{1,0:T(8,128)} %slots_768_1.6.refs_2_), custom_call_target="tpu_custom_call" | custom-call | flops 4831838208 | bytes 4194304 | tf_op jit(solution)/shard_map/slots_768_1/pallas_call | solution.py:215
  214.8 14.2 %slots_256_2.1.refs_8_ = f32[1024,256]{1,0:T(8,128)} custom-call(s32[10]{0:T(128)} %stack.61.table_ref, f32[2,1,1024,4096]{3,2,1,0:T(8,128)} %a_ref.13, f32[1024,256]{1,0:T(8,128)} %collective-permute-done.15.refs_0_.refs_1_, f32[1024,256]{1,0:T(8,128)} %collective-permute-done.15.refs_0_.refs_1_, ...), custom_call_target="tpu_custom_call" | custom-call | flops 3221225472 | bytes 8388608 | tf_op jit(solution)/shard_map/slots_256_2/pallas_call | solution.py:215
  229.1 4.9 %collective-permute-done.18.refs_6_.refs_7_ = f32[1024,256]{1,0:T(8,128)} collective-permute-done((f32[1024,256]{1,0:T(8,128)}, f32[1024,256]{1,0:T(8,128)}, u32[]{:S(2)}, u32[]{:S(2)}) %collective-permute-start.18) | collective-permute-done | bytes 1048608 | tf_op jit(solution)/shard_map/ppermute | solution.py:310
  233.9 3.9 %collective-permute-start.23 = (f32[256,384]{1,0:T(8,128)S(1)}, f32[256,384]{1,0:T(8,128)S(1)}, u32[]{:S(2)}, u32[]{:S(2)}) collective-permute-start(f32[256,384]{1,0:T(8,128)S(1)} %add.28), channel_id=1, source_target_pairs={{0,8},{2,10},{4,12},{6,14},{8,0},{10,2},{12,4},{14,6},{1,9},{3,11}... | collective-permute-start | bytes 1179656 | tf_op jit(solution)/shard_map/ppermute | solution.py:393
  237.9 9.7 %slots_256_1.3 = (f32[1024,128]{1,0:T(8,128)}, f32[1024,128]{1,0:T(8,128)}) custom-call(s32[10]{0:T(128)} %stack.61.table_ref, f32[2,1,1024,4096]{3,2,1,0:T(8,128)} %a_ref.13, f32[1024,256]{1,0:T(8,128)} %collective-permute-done.17.refs_4_.refs_5_.refs_0_.refs_1_, f32[1024,256]{1,0:T(8,128)} %collective-permute-done.17.refs_4_.refs_5_.refs_0_.refs_1_, ...), custom_call_target="tpu_custom_call" | custom-call | flops 1610612736 | bytes 4194304 | tf_op jit(solution)/shard_map/slots_256_1/pallas_call | solution.py:215
  247.7 7.6 %collective-permute-done.23 = f32[256,384]{1,0:T(8,128)S(1)} collective-permute-done((f32[256,384]{1,0:T(8,128)S(1)}, f32[256,384]{1,0:T(8,128)S(1)}, u32[]{:S(2)}, u32[]{:S(2)}) %collective-permute-start.23) | collective-permute-done | bytes 393248 | tf_op jit(solution)/shard_map/ppermute | solution.py:393
  265.8 3.4 %collective-permute-done.26 = f32[256,128]{1,0:T(8,128)S(1)} collective-permute-done((f32[256,128]{1,0:T(8,128)S(1)}, f32[256,128]{1,0:T(8,128)S(1)}, u32[]{:S(2)}, u32[]{:S(2)}) %collective-permute-start.26) | collective-permute-done | bytes 131104 | tf_op jit(solution)/shard_map/ppermute | solution.py:393
  269.2 3.4 %collective-permute-start.27 = (f32[256,128]{1,0:T(8,128)S(1)}, f32[256,128]{1,0:T(8,128)S(1)}, u32[]{:S(2)}, u32[]{:S(2)}) collective-permute-start(f32[256,128]{1,0:T(8,128)S(1)} %add.32), channel_id=1, source_target_pairs={{0,8},{2,10},{4,12},{6,14},{8,0},{10,2},{12,4},{14,6},{1,9},{3,11}... | collective-permute-start | bytes 393224 | tf_op jit(solution)/shard_map/ppermute | solution.py:393
  272.7 4.3 %collective-permute-done.27 = f32[256,128]{1,0:T(8,128)S(1)} collective-permute-done((f32[256,128]{1,0:T(8,128)S(1)}, f32[256,128]{1,0:T(8,128)S(1)}, u32[]{:S(2)}, u32[]{:S(2)}) %collective-permute-start.27) | collective-permute-done | bytes 131104 | tf_op jit(solution)/shard_map/ppermute | solution.py:393
  (88 shorter events, 66.3 us)
Async XLA Ops:
  7.2 11.4 %collective-permute-start.3 = (f32[2,512,256]{2,1,0:T(8,128)}, f32[2,512,256]{2,1,0:T(8,128)S(1)}, u32[]{:S(2)}, u32[]{:S(2)}) collective-permute-start(f32[2,512,256]{2,1,0:T(8,128)} %slice_select_fusion), channel_id=1, source_target_pairs={{0,1},{1,0},{2,3},{3,2},{4,5},{5,4},{6,7},{7,6},{8,9},{9,8},{10,11... | collective-permute-start | bytes 3145736 | tf_op jit(solution)/shard_map/ppermute | solution.py:317
  7.7 49.1 %collective-permute-start.2 = (f32[512,768]{1,0:T(8,128)}, f32[512,768]{1,0:T(8,128)}, u32[]{:S(2)}, u32[]{:S(2)}) collective-permute-start(f32[512,768]{1,0:T(8,128)} %get-tuple-element.83.refs_0_), channel_id=1, source_target_pairs={{0,2},{2,0},{4,6},{6,4},{8,10},{10,8},{12,14},{14,12},{1,3},{3,1},... | collective-permute-start | bytes 4718600 | tf_op jit(solution)/shard_map/ppermute | solution.py:314
  10.2 46.6 %collective-permute-start.1 = (f32[512,768]{1,0:T(8,128)}, f32[512,768]{1,0:T(8,128)}, u32[]{:S(2)}, u32[]{:S(2)}) collective-permute-start(f32[512,768]{1,0:T(8,128)} %get-tuple-element.83.refs_0_), channel_id=1, source_target_pairs={{0,4},{2,6},{4,8},{6,10},{8,12},{10,14},{1,5},{3,7},{5,9},{7,11},{... | collective-permute-start | bytes 4718600 | tf_op jit(solution)/shard_map/ppermute | solution.py:306
  14.8 42.0 %collective-permute-start = (f32[512,768]{1,0:T(8,128)}, f32[512,768]{1,0:T(8,128)}, u32[]{:S(2)}, u32[]{:S(2)}) collective-permute-start(f32[512,768]{1,0:T(8,128)} %get-tuple-element.83.refs_0_), channel_id=1, source_target_pairs={{4,0},{6,2},{8,4},{10,6},{12,8},{14,10},{5,1},{7,3},{9,5},{11,7},{... | collective-permute-start | bytes 4718600 | tf_op jit(solution)/shard_map/ppermute | solution.py:310
  16.1 40.7 %collective-permute-start.4 = (f32[512,256]{1,0:T(8,128)}, f32[512,256]{1,0:T(8,128)}, u32[]{:S(2)}, u32[]{:S(2)}) collective-permute-start(f32[512,256]{1,0:T(8,128)} %get-tuple-element.90), channel_id=1, source_target_pairs={{0,2},{2,0},{4,6},{6,4},{8,10},{10,8},{12,14},{14,12},{1,3},{3,1},... | collective-permute-start | bytes 1572872 | tf_op jit(solution)/shard_map/ppermute | solution.py:314
  59.6 36.5 %collective-permute-start.7 = (f32[512,768]{1,0:T(8,128)}, f32[512,768]{1,0:T(8,128)}, u32[]{:S(2)}, u32[]{:S(2)}) collective-permute-start(f32[512,768]{1,0:T(8,128)} %broadcast_select_fusion.refs_0_), channel_id=1, source_target_pairs={{0,2},{2,0},{4,6},{6,4},{8,10},{10,8},{12,14},{14,12},{1,3},{3,1},... | collective-permute-start | bytes 4718600 | tf_op jit(solution)/shard_map/ppermute | solution.py:314
  61.3 34.8 %collective-permute-start.6 = (f32[512,768]{1,0:T(8,128)}, f32[512,768]{1,0:T(8,128)}, u32[]{:S(2)}, u32[]{:S(2)}) collective-permute-start(f32[512,768]{1,0:T(8,128)} %collective-permute-done.1), channel_id=1, source_target_pairs={{4,8},{6,10},{8,12},{10,14},{5,9},{7,11},{9,13},{11,15},{20,24},{2... | collective-permute-start | bytes 4718600 | tf_op jit(solution)/shard_map/ppermute | solution.py:306
  63.2 40.3 %collective-permute-start.5 = (f32[512,768]{1,0:T(8,128)}, f32[512,768]{1,0:T(8,128)}, u32[]{:S(2)}, u32[]{:S(2)}) collective-permute-start(f32[512,768]{1,0:T(8,128)} %collective-permute-done.refs_2_), channel_id=1, source_target_pairs={{4,0},{6,2},{8,4},{10,6},{5,1},{7,3},{9,5},{11,7},{20,16},{22,18},... | collective-permute-start | bytes 4718600 | tf_op jit(solution)/shard_map/ppermute | solution.py:310
  103.5 36.8 %collective-permute-start.10 = (f32[512,768]{1,0:T(8,128)}, f32[512,768]{1,0:T(8,128)}, u32[]{:S(2)}, u32[]{:S(2)}) collective-permute-start(f32[512,768]{1,0:T(8,128)} %collective-permute-done.refs_2_), channel_id=1, source_target_pairs={{4,6},{6,4},{8,10},{10,8},{5,7},{7,5},{9,11},{11,9},{20,22},{22,20... | collective-permute-start | bytes 4718600 | tf_op jit(solution)/shard_map/ppermute | solution.py:314
  105.3 37.0 %collective-permute-start.11 = (f32[512,768]{1,0:T(8,128)}, f32[512,768]{1,0:T(8,128)}, u32[]{:S(2)}, u32[]{:S(2)}) collective-permute-start(f32[512,768]{1,0:T(8,128)} %collective-permute-done.5.refs_4_), channel_id=1, source_target_pairs={{0,2},{2,0},{1,3},{3,1},{16,18},{18,16},{17,19},{19,17}} | collective-permute-start | bytes 4718600 | tf_op jit(solution)/shard_map/ppermute | solution.py:314
  107.8 36.8 %collective-permute-start.8 = (f32[512,768]{1,0:T(8,128)}, f32[512,768]{1,0:T(8,128)}, u32[]{:S(2)}, u32[]{:S(2)}) collective-permute-start(f32[512,768]{1,0:T(8,128)} %collective-permute-done.5.refs_4_), channel_id=1, source_target_pairs={{4,0},{6,2},{5,1},{7,3},{20,16},{22,18},{21,17},{23,19}} | collective-permute-start | bytes 4718600 | tf_op jit(solution)/shard_map/ppermute | solution.py:310
  109.1 35.5 %collective-permute-start.12 = (f32[512,768]{1,0:T(8,128)}, f32[512,768]{1,0:T(8,128)}, u32[]{:S(2)}, u32[]{:S(2)}) collective-permute-start(f32[512,768]{1,0:T(8,128)} %collective-permute-done.6.refs_0_), channel_id=1, source_target_pairs={{12,14},{14,12},{13,15},{15,13},{28,30},{30,28},{29,31},{31,29}} | collective-permute-start | bytes 4718600 | tf_op jit(solution)/shard_map/ppermute | solution.py:314
  111.0 33.6 %collective-permute-start.9 = (f32[512,768]{1,0:T(8,128)}, f32[512,768]{1,0:T(8,128)}, u32[]{:S(2)}, u32[]{:S(2)}) collective-permute-start(f32[512,768]{1,0:T(8,128)} %collective-permute-done.6.refs_0_), channel_id=1, source_target_pairs={{8,12},{10,14},{9,13},{11,15},{24,28},{26,30},{25,29},{27,31}} | collective-permute-start | bytes 4718600 | tf_op jit(solution)/shard_map/ppermute | solution.py:306
  147.5 33.9 %collective-permute-start.13 = (f32[512,768]{1,0:T(8,128)}, f32[512,768]{1,0:T(8,128)}, u32[]{:S(2)}, u32[]{:S(2)}) collective-permute-start(f32[512,768]{1,0:T(8,128)} %select_select_fusion.refs_0_), channel_id=1, source_target_pairs={{0,2},{2,0},{4,6},{6,4},{8,10},{10,8},{12,14},{14,12},{1,3},{3,1},... | collective-permute-start | bytes 4718600 | tf_op jit(solution)/shard_map/ppermute | solution.py:314
  149.0 22.5 %collective-permute-start.15 = (f32[1024,256]{1,0:T(8,128)}, f32[1024,256]{1,0:T(8,128)}, u32[]{:S(2)}, u32[]{:S(2)}) collective-permute-start(f32[1024,256]{1,0:T(8,128)} %pad_maximum_fusion.2.refs_0_.refs_1_), channel_id=1, source_target_pairs={{0,4},{2,6},{4,8},{6,10},{8,12},{10,14},{1,5},{3,7},{5,9},{7,11},{... | collective-permute-start | bytes 3145736 | tf_op jit(solution)/shard_map/ppermute | solution.py:306
  151.9 24.7 %collective-permute-start.14 = (f32[1024,256]{1,0:T(8,128)}, f32[1024,256]{1,0:T(8,128)}, u32[]{:S(2)}, u32[]{:S(2)}) collective-permute-start(f32[1024,256]{1,0:T(8,128)} %pad_maximum_fusion.2.refs_0_.refs_1_), channel_id=1, source_target_pairs={{4,0},{6,2},{8,4},{10,6},{12,8},{14,10},{5,1},{7,3},{9,5},{11,7},{... | collective-permute-start | bytes 3145736 | tf_op jit(solution)/shard_map/ppermute | solution.py:310
  181.4 23.7 %collective-permute-start.16 = (f32[1024,256]{1,0:T(8,128)}, f32[1024,256]{1,0:T(8,128)}, u32[]{:S(2)}, u32[]{:S(2)}) collective-permute-start(f32[1024,256]{1,0:T(8,128)} %collective-permute-done.14.refs_2_.refs_3_.refs_6_.refs_7_), channel_id=1, source_target_pairs={{4,0},{6,2},{8,4},{10,6},{5,1},{7,3},{9,5},{11,7},{20,16},{22,18},... | collective-permute-start | bytes 3145736 | tf_op jit(solution)/shard_map/ppermute | solution.py:310
  182.7 22.4 %collective-permute-start.17 = (f32[1024,256]{1,0:T(8,128)}, f32[1024,256]{1,0:T(8,128)}, u32[]{:S(2)}, u32[]{:S(2)}) collective-permute-start(f32[1024,256]{1,0:T(8,128)} %collective-permute-done.15.refs_0_.refs_1_), channel_id=1, source_target_pairs={{4,8},{6,10},{8,12},{10,14},{5,9},{7,11},{9,13},{11,15},{20,24},{2... | collective-permute-start | bytes 3145736 | tf_op jit(solution)/shard_map/ppermute | solution.py:306
  205.1 28.9 %collective-permute-start.18 = (f32[1024,256]{1,0:T(8,128)}, f32[1024,256]{1,0:T(8,128)}, u32[]{:S(2)}, u32[]{:S(2)}) collective-permute-start(f32[1024,256]{1,0:T(8,128)} %collective-permute-done.16.refs_8_.refs_9_.refs_4_.refs_5_), channel_id=1, source_target_pairs={{4,0},{6,2},{5,1},{7,3},{20,16},{22,18},{21,17},{23,19}} | collective-permute-start | bytes 3145736 | tf_op jit(solution)/shard_map/ppermute | solution.py:310
  206.4 27.6 %collective-permute-start.19 = (f32[1024,256]{1,0:T(8,128)}, f32[1024,256]{1,0:T(8,128)}, u32[]{:S(2)}, u32[]{:S(2)}) collective-permute-start(f32[1024,256]{1,0:T(8,128)} %collective-permute-done.17.refs_4_.refs_5_.refs_0_.refs_1_), channel_id=1, source_target_pairs={{8,12},{10,14},{9,13},{11,15},{24,28},{26,30},{25,29},{27,31}} | collective-permute-start | bytes 3145736 | tf_op jit(solution)/shard_map/ppermute | solution.py:306
  213.3 15.8 %collective-permute-start.21 = (f32[256,384]{1,0:T(8,128)S(1)}, f32[256,384]{1,0:T(8,128)S(1)}, u32[]{:S(2)}, u32[]{:S(2)}) collective-permute-start(f32[256,384]{1,0:T(8,128)S(1)} %get-tuple-element.142), channel_id=1, source_target_pairs={{0,2},{2,0},{4,6},{6,4},{8,10},{10,8},{12,14},{14,12},{1,3},{3,1},... | collective-permute-start | bytes 1179656 | tf_op jit(solution)/shard_map/ppermute | solution.py:393
  233.9 21.4 %collective-permute-start.23 = (f32[256,384]{1,0:T(8,128)S(1)}, f32[256,384]{1,0:T(8,128)S(1)}, u32[]{:S(2)}, u32[]{:S(2)}) collective-permute-start(f32[256,384]{1,0:T(8,128)S(1)} %add.28), channel_id=1, source_target_pairs={{0,8},{2,10},{4,12},{6,14},{8,0},{10,2},{12,4},{14,6},{1,9},{3,11}... | collective-permute-start | bytes 1179656 | tf_op jit(solution)/shard_map/ppermute | solution.py:393
  247.6 8.6 %collective-permute-start.22 = (f32[1024,128]{1,0:T(8,128)}, f32[1024,128]{1,0:T(8,128)S(1)}, u32[]{:S(2)}, u32[]{:S(2)}) collective-permute-start(f32[1024,128]{1,0:T(8,128)} %get-tuple-element.152), channel_id=1, source_target_pairs={{0,1},{1,0},{2,3},{3,2},{4,5},{5,4},{6,7},{7,6},{8,9},{9,8},{10,11... | collective-permute-start | bytes 1572872 | tf_op jit(solution)/shard_map/ppermute | solution.py:317
  255.3 10.3 %collective-permute-start.24 = (f32[256,384]{1,0:T(8,128)S(1)}, f32[256,384]{1,0:T(8,128)S(1)}, u32[]{:S(2)}, u32[]{:S(2)}) collective-permute-start(f32[256,384]{1,0:T(8,128)S(1)} %add.29), channel_id=1, source_target_pairs={{0,4},{2,6},{4,0},{6,2},{8,12},{10,14},{12,8},{14,10},{1,5},{3,7},... | collective-permute-start | bytes 1179656 | tf_op jit(solution)/shard_map/ppermute | solution.py:393
  (13 other events, 77.3 us)
